TPU v7x, 256 devices: a whole 4x4x8 slice. The times are simulated.
256 devices in a mesh: dp: 16 (over z_lo, y), mp: 16 (over z_hi, x, core).
Axes of the slice: x: 4, y: 4, z: 8 (z_hi: 2, z_lo: 4; z = z_hi * 4 + z_lo), core: 2. Of those that a mesh axis runs over, the one named last changes fastest.
Arguments:
- context: bfloat16 [8192, 6144], P('dp', 'mp'), may hold values from -6 to 6
- w_out: bfloat16 [6144, 6144], P('mp'), may hold values from -0.078125 to 0.078125
- residual: bfloat16 [8192, 6144], P(('dp', 'mp')), may hold values from -6 to 6
- gain: float32 [6144], replicated, may hold values from 0.5 to 1.5
- cotangent: bfloat16 [8192, 6144], P(('dp', 'mp')), may hold values from -6 to 6
Outputs:
- normed: bfloat16 [8192, 6144], P(('dp', 'mp'))
- residual_stream_gradient: bfloat16 [8192, 6144], P(('dp', 'mp'))
- context_grad: bfloat16 [8192, 6144], P('dp', 'mp')
- weight_grad: float32 [6144, 6144], P('mp', 'dp')
All inputs are finite; a program needn't handle non-finite values.
Results may differ from a plain program's by a relative error of at most 0.015.
Values may be sent and summed in bfloat16 or wider, within the bound.
No kernel may reach another device: no remote copies, remote signals or barrier semaphores. Data moves between devices by JAX's collectives and lax.ppermute only.
A program may use at most 128 MiB of HBM per device.

v0:
```python
import math

import jax
import jax.numpy as jnp
from jax import lax
from jax.experimental import pallas as pl
from jax.experimental.pallas import tpu as pltpu
from jax.sharding import PartitionSpec as P

F32 = jnp.float32
BF16 = jnp.bfloat16
DX = (1, 2, 3, 0)
ORDER = [(dz, dc, dx) for dz in (1, 0) for dc in (1, 0) for dx in DX]


def mp_perm(dz=0, dx=0, dc=0):
    pairs = []
    for m in range(16):
        zh, x, c = m // 8, (m // 2) % 4, m % 2
        pairs.append((m, (zh ^ dz) * 8 + ((x + dx) % 4) * 2 + (c ^ dc)))
    return pairs


def to_core(a):
    return lax.ppermute(a, "mp", mp_perm(dc=1))


def to_z(a):
    return lax.ppermute(a, "mp", mp_perm(dz=1))


def to_x(a, dx):
    return lax.ppermute(a, "mp", mp_perm(dx=dx))


def add(*terms):
    total = terms[0].astype(F32)
    for t in terms[1:]:
        total = total + t.astype(F32)
    return total


def project_kernel(a_ref, w_ref, other_ref, own_ref):
    n = other_ref.shape[0]
    out = jnp.dot(a_ref[...], w_ref[...], preferred_element_type=F32).astype(BF16)
    other_ref[...] = out[:n]
    own_ref[...] = out[n:]


def project(a, w):
    rows, width = a.shape
    features = w.shape[1]
    tile = min(1024, features)
    half = jax.ShapeDtypeStruct((rows // 2, features), BF16)
    out_spec = pl.BlockSpec((rows // 2, tile), lambda i: (0, i))
    return pl.pallas_call(
        project_kernel,
        grid=(features // tile,),
        in_specs=[pl.BlockSpec((rows, width), lambda i: (0, 0)), pl.BlockSpec((width, tile), lambda i: (0, i))],
        out_specs=[out_spec, out_spec],
        out_shape=[half, half],
        cost_estimate=pl.CostEstimate(
            flops=2 * rows * width * features, bytes_accessed=2 * features * (rows + width), transcendentals=0
        ),
    )(a, w)


def reduce_x(q):
    r = q.shape[0] // 4
    b1, b2, b3, b0 = (q[i * r : (i + 1) * r] for i in range(4))
    return add(b0, to_x(b1, 1), to_x(b2, 2), to_x(b3, 3))


def gather_x(b):
    return [to_x(b, 3), to_x(b, 2), to_x(b, 1), b]


def contract_rows(a, b):
    return lax.dot_general(a, b, (((0,), (0,)), ((), ())), preferred_element_type=F32)


def contract_columns(a, b):
    return lax.dot_general(a, b, (((1,), (1,)), ((), ())), preferred_element_type=F32)


def by_image(blocks):
    r = blocks[0].shape[0] // 16
    parts = [b.reshape(16, r, -1) for b in blocks]
    return jnp.concatenate(parts, axis=1).reshape(16 * r * len(blocks), -1)


def per_device(context, w_out, residual, gain, cotangent):
    rows, width = context.shape
    r, quarter = rows // 16, rows // 4
    row_factor = 1.0 / math.sqrt(rows * 16)
    me = lax.axis_index("mp")
    zh, x, c = me // 8, (me // 2) % 4, me % 2
    idx = jnp.stack([(zh ^ dz) * 8 + ((x + dx) % 4) * 2 + (c ^ dc) for dz, dc, dx in ORDER])
    ctx = context.reshape(16, r, width)[idx].reshape(4, quarter, width)

    other0, own0 = project(ctx[:2].reshape(2 * quarter, width), w_out)
    q0 = add(own0, to_core(other0)).astype(BF16)
    other1, own1 = project(ctx[2:].reshape(2 * quarter, width), w_out)
    q1 = add(own1, to_core(other1)).astype(BF16)
    z0 = to_z(reduce_x(q0).astype(BF16))
    mixed = reduce_x(q1)

    there = to_core(ctx[::2].reshape(2 * quarter, width))
    ctx_far = lax.all_gather(jnp.concatenate([ctx[1], there[:quarter]], axis=1), "dp", axis=0, tiled=True)
    ctx_near = lax.all_gather(jnp.concatenate([ctx[3], there[quarter:]], axis=1), "dp", axis=0, tiled=True)
    w_sibling = to_core(w_out)

    presum = mixed + z0.astype(F32) + residual.astype(F32)
    average = jnp.mean(presum, axis=-1, keepdims=True)
    centered = presum - average
    inverse = lax.rsqrt(jnp.mean(centered * centered, axis=-1, keepdims=True) + 1e-06)
    xhat = centered * inverse
    normed = (xhat * gain).astype(BF16)
    scaled = cotangent.astype(F32) * gain
    first = jnp.mean(scaled, axis=-1, keepdims=True)
    second = jnp.mean(scaled * xhat, axis=-1, keepdims=True)
    grad = (inverse * (scaled - first - xhat * second)).astype(BF16)

    near = gather_x(grad)
    far = gather_x(to_z(grad))
    blocks = grad.reshape(r, 16, width).transpose(1, 0, 2).reshape(rows, width)
    turned = lax.all_to_all(blocks, "dp", 0, 0, tiled=True)
    turned_near = gather_x(turned)
    turned_far = gather_x(to_z(turned))

    gathered = jnp.concatenate(far + near, axis=0)
    cg_own = contract_columns(gathered, w_out).astype(BF16)
    cg_sibling = contract_columns(gathered, w_sibling).astype(BF16)
    cg = jnp.concatenate([to_core(cg_sibling), cg_own], axis=0)
    pos = [
        (1 - ((m % 2) ^ c)) * 8 + (1 - ((m // 8) ^ zh)) * 4 + ((m // 2) % 4 - x + 3) % 4 for m in range(16)
    ]
    context_grad = cg.reshape(16, r, width)[jnp.stack(pos)].reshape(rows, width)

    wg_near = contract_rows(ctx_near, by_image(turned_near))
    turned_far, wg_near, context_grad = lax.optimization_barrier((turned_far, wg_near, context_grad))
    wg = wg_near + contract_rows(ctx_far, by_image(turned_far))
    weight_grad = (wg[:width] + to_core(wg[width:])) * row_factor
    return (normed, grad, context_grad, weight_grad)


def solution(mesh):
    return jax.shard_map(
        per_device,
        mesh=mesh,
        in_specs=(P("dp", "mp"), P("mp", None), P(("dp", "mp"), None), P(), P(("dp", "mp"), None)),
        out_specs=(P(("dp", "mp"), None), P(("dp", "mp"), None), P("dp", "mp"), P("mp", "dp")),
        check_vma=False,
    )
```

profile of v0, /device:TPU:1, one launch (start us, length us, event | category | flops | bytes accessed | tf_op | source)
XLA Modules:
  0.0 239.4 jit_solution(15112148462247487289)
XLA Ops:
  9.6 6.6 %shard_map.85 = (bf16[128,6144]{1,0:T(8,128)(2,1)}, bf16[128,6144]{1,0:T(8,128)(2,1)}) custom-call(bf16[256,384]{1,0:T(8,128)(2,1)} %bitcast.81, bf16[384,6144]{1,0:T(8,128)(2,1)} %w_ref.3), custom_call_target="tpu_custom_call" | custom-call | flops 1207959552 | bytes 7864320 | tf_op jit(solution)/shard_map/pallas_call | solution.py:56
  16.2 3.2 %collective-permute-start.4 = (bf16[128,6144]{1,0:T(8,128)(2,1)}, bf16[128,6144]{1,0:T(8,128)(2,1)}, u32[]{:S(2)}, u32[]{:S(2)}) collective-permute-start(bf16[128,6144]{1,0:T(8,128)(2,1)} %get-tuple-element.17), channel_id=1, source_target_pairs={{0,1},{1,0},{2,3},{3,2},{4,5},{5,4},{6,7},{7,6},{8,9},{9,8},{10,11... | collective-permute-start | bytes 4718600 | tf_op jit(solution)/shard_map/ppermute | solution.py:25
  19.4 6.6 %shard_map.84 = (bf16[128,6144]{1,0:T(8,128)(2,1)}, bf16[128,6144]{1,0:T(8,128)(2,1)}) custom-call(bf16[256,384]{1,0:T(8,128)(2,1)} %bitcast.80, bf16[384,6144]{1,0:T(8,128)(2,1)} %w_ref.3), custom_call_target="tpu_custom_call" | custom-call | flops 1207959552 | bytes 7864320 | tf_op jit(solution)/shard_map/pallas_call | solution.py:56
  26.6 2.7 %collective-permute-done.13 = bf16[256,384]{1,0:T(8,128)(2,1)S(1)} collective-permute-done((bf16[256,384]{1,0:T(8,128)(2,1)S(1)}, bf16[256,384]{1,0:T(8,128)(2,1)S(1)}, u32[]{:S(2)}, u32[]{:S(2)}) %collective-permute-start.13) | collective-permute-done | bytes 196640 | tf_op jit(solution)/shard_map/ppermute | solution.py:25
  30.1 2.4 add_convert_fusion
  32.7 1.9 collective-permute-start.6
  36.7 1.8 collective-permute-start.2
  38.4 6.6 %collective-permute-done.5 = bf16[32,6144]{1,0:T(8,128)(2,1)S(1)} collective-permute-done((bf16[32,6144]{1,0:T(8,128)(2,1)S(1)}, bf16[32,6144]{1,0:T(8,128)(2,1)S(1)}, u32[]{:S(2)}, u32[]{:S(2)}) %collective-permute-start.5) | collective-permute-done | bytes 393248 | tf_op jit(solution)/shard_map/ppermute | solution.py:33
  45.0 7.1 %collective-permute-done.6 = bf16[32,6144]{1,0:T(8,128)(2,1)S(1)} collective-permute-done((bf16[32,6144]{1,0:T(8,128)(2,1)S(1)}, bf16[32,6144]{1,0:T(8,128)(2,1)S(1)}, u32[]{:S(2)}, u32[]{:S(2)}) %collective-permute-start.6) | collective-permute-done | bytes 393248 | tf_op jit(solution)/shard_map/ppermute | solution.py:33
  53.6 5.6 %collective-permute-start.8 = (bf16[32,6144]{1,0:T(8,128)(2,1)S(1)}, bf16[32,6144]{1,0:T(8,128)(2,1)S(1)}, u32[]{:S(2)}, u32[]{:S(2)}) collective-permute-start(bf16[32,6144]{1,0:T(8,128)(2,1)S(1)} %add_convert_fusion.2), channel_id=1, source_target_pairs={{0,8},{1,9},{2,10},{3,11},{4,12},{5,13},{6,14},{7,15},{8,0},{9,1},... | collective-permute-start | bytes 1179656 | tf_op jit(solution)/shard_map/ppermute | solution.py:29
  59.2 2.7 %collective-permute-done.1 = bf16[32,6144]{1,0:T(8,128)(2,1)S(1)} collective-permute-done((bf16[32,6144]{1,0:T(8,128)(2,1)S(1)}, bf16[32,6144]{1,0:T(8,128)(2,1)S(1)}, u32[]{:S(2)}, u32[]{:S(2)}) %collective-permute-start.1) | collective-permute-done | bytes 393248 | tf_op jit(solution)/shard_map/ppermute | solution.py:33
  61.9 7.0 %collective-permute-done.2 = bf16[32,6144]{1,0:T(8,128)(2,1)S(1)} collective-permute-done((bf16[32,6144]{1,0:T(8,128)(2,1)S(1)}, bf16[32,6144]{1,0:T(8,128)(2,1)S(1)}, u32[]{:S(2)}, u32[]{:S(2)}) %collective-permute-start.2) | collective-permute-done | bytes 393248 | tf_op jit(solution)/shard_map/ppermute | solution.py:33
  70.0 4.2 %collective-permute-done.8 = bf16[32,6144]{1,0:T(8,128)(2,1)S(1)} collective-permute-done((bf16[32,6144]{1,0:T(8,128)(2,1)S(1)}, bf16[32,6144]{1,0:T(8,128)(2,1)S(1)}, u32[]{:S(2)}, u32[]{:S(2)}) %collective-permute-start.8) | collective-permute-done | bytes 393248 | tf_op jit(solution)/shard_map/ppermute | solution.py:29
  76.3 5.3 %collective-permute-start.17 = (bf16[32,6144]{1,0:T(8,128)(2,1)S(1)}, bf16[32,6144]{1,0:T(8,128)(2,1)S(1)}, u32[]{:S(2)}, u32[]{:S(2)}) collective-permute-start(bf16[32,6144]{1,0:T(8,128)(2,1)S(1)} %get-tuple-element.34), channel_id=1, source_target_pairs={{0,8},{1,9},{2,10},{3,11},{4,12},{5,13},{6,14},{7,15},{8,0},{9,1},... | collective-permute-start | bytes 1179656 | tf_op jit(solution)/shard_map/ppermute | solution.py:29
  81.6 4.2 %collective-permute-start.24 = (bf16[384,6144]{1,0:T(8,128)(2,1)}, bf16[384,6144]{1,0:T(8,128)(2,1)}, u32[]{:S(2)}, u32[]{:S(2)}) collective-permute-start(bf16[384,6144]{1,0:T(8,128)(2,1)} %w_ref.3), channel_id=1, source_target_pairs={{0,1},{1,0},{2,3},{3,2},{4,5},{5,4},{6,7},{7,6},{8,9},{9,8},{10,11... | collective-permute-start | bytes 14155784 | tf_op jit(solution)/shard_map/ppermute | solution.py:25
  86.0 17.2 %collective-permute-done.17 = bf16[32,6144]{1,0:T(8,128)(2,1)S(1)} collective-permute-done((bf16[32,6144]{1,0:T(8,128)(2,1)S(1)}, bf16[32,6144]{1,0:T(8,128)(2,1)S(1)}, u32[]{:S(2)}, u32[]{:S(2)}) %collective-permute-start.17) | collective-permute-done | bytes 393248 | tf_op jit(solution)/shard_map/ppermute | solution.py:29
  103.2 3.5 %collective-permute-start.18 = (bf16[32,6144]{1,0:T(8,128)(2,1)S(1)}, bf16[32,6144]{1,0:T(8,128)(2,1)S(1)}, u32[]{:S(2)}, u32[]{:S(2)}) collective-permute-start(bf16[32,6144]{1,0:T(8,128)(2,1)S(1)} %collective-permute-done.17), channel_id=1, source_target_pairs={{0,6},{1,7},{2,0},{3,1},{4,2},{5,3},{6,4},{7,5},{8,14},{9,15},{10,... | collective-permute-start | bytes 1179656 | tf_op jit(solution)/shard_map/ppermute | solution.py:33
  110.0 20.3 %all-to-all-start = ((bf16[16,32,384]{2,1,0:T(8,128)(2,1)}), bf16[16,32,384]{2,1,0:T(8,128)(2,1)S(1)}, u32[]{:S(2)}, u32[]{:S(2)}) async-start(bf16[16,32,384]{2,1,0:T(8,128)(2,1)} %bitcast.69), calls=%async_computation | async-start | bytes 786432 | tf_op jit(solution)/shard_map/all_to_all | solution.py:127
  130.3 3.7 %collective-permute-start.19 = (bf16[32,6144]{1,0:T(8,128)(2,1)S(1)}, bf16[32,6144]{1,0:T(8,128)(2,1)S(1)}, u32[]{:S(2)}, u32[]{:S(2)}) collective-permute-start(bf16[32,6144]{1,0:T(8,128)(2,1)S(1)} %collective-permute-done.17), channel_id=1, source_target_pairs={{0,4},{1,5},{2,6},{3,7},{4,0},{5,1},{6,2},{7,3},{8,12},{9,13},{10,... | collective-permute-start | bytes 1179656 | tf_op jit(solution)/shard_map/ppermute | solution.py:33
  134.7 6.1 %collective-permute-done.19 = bf16[32,6144]{1,0:T(8,128)(2,1)S(1)} collective-permute-done((bf16[32,6144]{1,0:T(8,128)(2,1)S(1)}, bf16[32,6144]{1,0:T(8,128)(2,1)S(1)}, u32[]{:S(2)}, u32[]{:S(2)}) %collective-permute-start.19) | collective-permute-done | bytes 393248 | tf_op jit(solution)/shard_map/ppermute | solution.py:33
  142.3 7.3 %collective-permute-done.20 = bf16[32,6144]{1,0:T(8,128)(2,1)S(1)} collective-permute-done((bf16[32,6144]{1,0:T(8,128)(2,1)S(1)}, bf16[32,6144]{1,0:T(8,128)(2,1)S(1)}, u32[]{:S(2)}, u32[]{:S(2)}) %collective-permute-start.20) | collective-permute-done | bytes 393248 | tf_op jit(solution)/shard_map/ppermute | solution.py:33
  151.3 2.9 %collective-permute-start.15 = (bf16[512,384]{1,0:T(8,128)(2,1)S(1)}, bf16[512,384]{1,0:T(8,128)(2,1)S(1)}, u32[]{:S(2)}, u32[]{:S(2)}) collective-permute-start(bf16[512,384]{1,0:T(8,128)(2,1)S(1)} %bitcast.76), channel_id=1, source_target_pairs={{0,4},{1,5},{2,6},{3,7},{4,0},{5,1},{6,2},{7,3},{8,12},{9,13},{10,... | collective-permute-start | bytes 1179656 | tf_op jit(solution)/shard_map/ppermute | solution.py:33
  155.7 3.3 %collective-permute-start.9 = (bf16[512,384]{1,0:T(8,128)(2,1)S(1)}, bf16[512,384]{1,0:T(8,128)(2,1)S(1)}, u32[]{:S(2)}, u32[]{:S(2)}) collective-permute-start(bf16[512,384]{1,0:T(8,128)(2,1)S(1)} %bitcast.78), channel_id=1, source_target_pairs={{0,8},{1,9},{2,10},{3,11},{4,12},{5,13},{6,14},{7,15},{8,0},{9,1},... | collective-permute-start | bytes 1179656 | tf_op jit(solution)/shard_map/ppermute | solution.py:29
  160.5 5.2 %convolution_convert_fusion.1 = bf16[256,384]{1,0:T(8,128)(2,1)S(1)} fusion(bf16[256,6144]{1,0:T(8,128)(2,1)} %constant_dynamic-update-slice_fusion, bf16[384,6144]{1,0:T(8,128)(2,1)} %collective-permute-done.24), kind=kOutput, calls=%fused_computation.7 | convolution fusion | flops 1208057856 | bytes 8060928 | tf_op jit(solution)/shard_map/dot_general | solution.py:83
  165.7 5.4 %collective-permute-start.25 = (bf16[256,384]{1,0:T(8,128)(2,1)S(1)}, bf16[256,384]{1,0:T(8,128)(2,1)S(1)}, u32[]{:S(2)}, u32[]{:S(2)}) collective-permute-start(bf16[256,384]{1,0:T(8,128)(2,1)S(1)} %convolution_convert_fusion.1), channel_id=1, source_target_pairs={{0,1},{1,0},{2,3},{3,2},{4,5},{5,4},{6,7},{7,6},{8,9},{9,8},{10,11... | collective-permute-start | bytes 589832 | tf_op jit(solution)/shard_map/ppermute | solution.py:25
  171.1 5.1 %convolution_convert_fusion = bf16[256,384]{1,0:T(8,128)(2,1)S(1)} fusion(bf16[256,6144]{1,0:T(8,128)(2,1)} %constant_dynamic-update-slice_fusion, bf16[384,6144]{1,0:T(8,128)(2,1)} %w_ref.3), kind=kOutput, calls=%fused_computation.6 | convolution fusion | flops 1208057856 | bytes 8060928 | tf_op jit(solution)/shard_map/dot_general | solution.py:83
  180.6 3.7 %fusion.10 = f32[768,384]{1,0:T(8,128)S(1)} fusion(bf16[2048,768]{1,0:T(8,128)(2,1)} %all-gather.3.cloned.1.call-done, bf16[2048,384]{1,0:T(8,128)(2,1)S(1)} %bitcast.71), kind=kOutput, calls=%fused_computation.47 | convolution fusion | flops 1207959552 | bytes 5898240 | tf_op jit(solution)/shard_map/dot_general | solution.py:79
  184.3 1.9 collective-permute-done.10
  187.6 11.4 %collective-permute-done.12 = bf16[512,384]{1,0:T(8,128)(2,1)} collective-permute-done((bf16[512,384]{1,0:T(8,128)(2,1)S(1)}, bf16[512,384]{1,0:T(8,128)(2,1)}, u32[]{:S(2)}, u32[]{:S(2)}) %collective-permute-start.12) | collective-permute-done | bytes 393248 | tf_op jit(solution)/shard_map/ppermute | solution.py:33
  200.5 17.3 %all-gather.5.cloned.1.call-done = bf16[2048,768]{1,0:T(8,128)(2,1)} async-done(((bf16[128,768]{1,0:T(8,128)(2,1)}), bf16[2048,768]{1,0:T(8,128)(2,1)}) %all-gather.5.cloned.1.call-update) | async-done | bytes 3145744 | tf_op jit(solution)/shard_map/all_gather | solution.py:109
  217.8 3.7 %fusion.11 = f32[768,384]{1,0:T(8,128)S(1)} fusion(bf16[2048,768]{1,0:T(8,128)(2,1)} %all-gather.5.cloned.1.call-done, bf16[2048,384]{1,0:T(8,128)(2,1)S(1)} %bitcast.72), kind=kOutput, calls=%fused_computation.48 | convolution fusion | flops 1207959552 | bytes 5898240 | tf_op jit(solution)/shard_map/dot_general | solution.py:79
  221.7 8.4 %collective-permute-start.26 = (f32[384,384]{1,0:T(8,128)S(1)}, f32[384,384]{1,0:T(8,128)S(1)}, u32[]{:S(2)}, u32[]{:S(2)}) collective-permute-start(f32[384,384]{1,0:T(8,128)S(1)} %slice.91), channel_id=1, source_target_pairs={{0,1},{1,0},{2,3},{3,2},{4,5},{5,4},{6,7},{7,6},{8,9},{9,8},{10,11... | collective-permute-start | bytes 1769480 | tf_op jit(solution)/shard_map/ppermute | solution.py:25
  (89 shorter events, 30.9 us)
Async XLA Ops:
  7.2 173.4 %all-gather.3.cloned.1.call-start = ((), (), s32[]{:S(2)}) async-start(), calls=%async_computation.1 | async-start | bytes 3342336 | tf_op jit(solution)/shard_map/all_gather | solution.py:110
  16.2 14.0 %collective-permute-start.4 = (bf16[128,6144]{1,0:T(8,128)(2,1)}, bf16[128,6144]{1,0:T(8,128)(2,1)}, u32[]{:S(2)}, u32[]{:S(2)}) collective-permute-start(bf16[128,6144]{1,0:T(8,128)(2,1)} %get-tuple-element.17), channel_id=1, source_target_pairs={{0,1},{1,0},{2,3},{3,2},{4,5},{5,4},{6,7},{7,6},{8,9},{9,8},{10,11... | collective-permute-start | bytes 4718600 | tf_op jit(solution)/shard_map/ppermute | solution.py:25
  26.0 9.8 %collective-permute-start = (bf16[128,6144]{1,0:T(8,128)(2,1)}, bf16[128,6144]{1,0:T(8,128)(2,1)S(1)}, u32[]{:S(2)}, u32[]{:S(2)}) collective-permute-start(bf16[128,6144]{1,0:T(8,128)(2,1)} %get-tuple-element.15), channel_id=1, source_target_pairs={{0,1},{1,0},{2,3},{3,2},{4,5},{5,4},{6,7},{7,6},{8,9},{9,8},{10,11... | collective-permute-start | bytes 4718600 | tf_op jit(solution)/shard_map/ppermute | solution.py:25
  26.0 3.3 %collective-permute-start.13 = (bf16[256,384]{1,0:T(8,128)(2,1)S(1)}, bf16[256,384]{1,0:T(8,128)(2,1)S(1)}, u32[]{:S(2)}, u32[]{:S(2)}) collective-permute-start(bf16[256,384]{1,0:T(8,128)(2,1)S(1)} %bitcast.89), channel_id=1, source_target_pairs={{0,1},{1,0},{2,3},{3,2},{4,5},{5,4},{6,7},{7,6},{8,9},{9,8},{10,11... | collective-permute-start | bytes 589832 | tf_op jit(solution)/shard_map/ppermute | solution.py:25
  30.1 187.7 %all-gather.5.cloned.1.call-start = ((), (), s32[]{:S(2)}) async-start(), calls=%async_computation.2 | async-start | bytes 3342336 | tf_op jit(solution)/shard_map/all_gather | solution.py:109
  32.6 12.4 %collective-permute-start.5 = (bf16[32,6144]{1,0:T(8,128)(2,1)S(1)}, bf16[32,6144]{1,0:T(8,128)(2,1)S(1)}, u32[]{:S(2)}, u32[]{:S(2)}) collective-permute-start(bf16[32,6144]{1,0:T(8,128)(2,1)S(1)} %get-tuple-element.31), channel_id=1, source_target_pairs={{0,2},{1,3},{2,4},{3,5},{4,6},{5,7},{6,0},{7,1},{8,10},{9,11},{10,... | collective-permute-start | bytes 1179656 | tf_op jit(solution)/shard_map/ppermute | solution.py:33
  32.7 19.3 %collective-permute-start.6 = (bf16[32,6144]{1,0:T(8,128)(2,1)S(1)}, bf16[32,6144]{1,0:T(8,128)(2,1)S(1)}, u32[]{:S(2)}, u32[]{:S(2)}) collective-permute-start(bf16[32,6144]{1,0:T(8,128)(2,1)S(1)} %get-tuple-element.33), channel_id=1, source_target_pairs={{0,4},{1,5},{2,6},{3,7},{4,0},{5,1},{6,2},{7,3},{8,12},{9,13},{10,... | collective-permute-start | bytes 1179656 | tf_op jit(solution)/shard_map/ppermute | solution.py:33
  34.6 18.8 %collective-permute-start.7 = (bf16[32,6144]{1,0:T(8,128)(2,1)S(1)}, bf16[32,6144]{1,0:T(8,128)(2,1)S(1)}, u32[]{:S(2)}, u32[]{:S(2)}) collective-permute-start(bf16[32,6144]{1,0:T(8,128)(2,1)S(1)} %get-tuple-element.32), channel_id=1, source_target_pairs={{0,6},{1,7},{2,0},{3,1},{4,2},{5,3},{6,4},{7,5},{8,14},{9,15},{10,... | collective-permute-start | bytes 1179656 | tf_op jit(solution)/shard_map/ppermute | solution.py:33
  36.2 38.7 %copy-start.3 = (bf16[32,6144]{1,0:T(8,128)(2,1)S(1)}, bf16[32,6144]{1,0:T(8,128)(2,1)}, u32[]{:S(2)}) copy-start(bf16[32,6144]{1,0:T(8,128)(2,1)} %param.9) | copy-start | bytes 1179652
  36.3 25.6 %collective-permute-start.1 = (bf16[32,6144]{1,0:T(8,128)(2,1)S(1)}, bf16[32,6144]{1,0:T(8,128)(2,1)S(1)}, u32[]{:S(2)}, u32[]{:S(2)}) collective-permute-start(bf16[32,6144]{1,0:T(8,128)(2,1)S(1)} %get-tuple-element.28), channel_id=1, source_target_pairs={{0,2},{1,3},{2,4},{3,5},{4,6},{5,7},{6,0},{7,1},{8,10},{9,11},{10,... | collective-permute-start | bytes 1179656 | tf_op jit(solution)/shard_map/ppermute | solution.py:33
  36.7 32.2 %collective-permute-start.2 = (bf16[32,6144]{1,0:T(8,128)(2,1)S(1)}, bf16[32,6144]{1,0:T(8,128)(2,1)S(1)}, u32[]{:S(2)}, u32[]{:S(2)}) collective-permute-start(bf16[32,6144]{1,0:T(8,128)(2,1)S(1)} %get-tuple-element.30), channel_id=1, source_target_pairs={{0,4},{1,5},{2,6},{3,7},{4,0},{5,1},{6,2},{7,3},{8,12},{9,13},{10,... | collective-permute-start | bytes 1179656 | tf_op jit(solution)/shard_map/ppermute | solution.py:33
  45.0 25.0 %collective-permute-start.3 = (bf16[32,6144]{1,0:T(8,128)(2,1)S(1)}, bf16[32,6144]{1,0:T(8,128)(2,1)S(1)}, u32[]{:S(2)}, u32[]{:S(2)}) collective-permute-start(bf16[32,6144]{1,0:T(8,128)(2,1)S(1)} %get-tuple-element.29), channel_id=1, source_target_pairs={{0,6},{1,7},{2,0},{3,1},{4,2},{5,3},{6,4},{7,5},{8,14},{9,15},{10,... | collective-permute-start | bytes 1179656 | tf_op jit(solution)/shard_map/ppermute | solution.py:33
  53.6 20.6 %collective-permute-start.8 = (bf16[32,6144]{1,0:T(8,128)(2,1)S(1)}, bf16[32,6144]{1,0:T(8,128)(2,1)S(1)}, u32[]{:S(2)}, u32[]{:S(2)}) collective-permute-start(bf16[32,6144]{1,0:T(8,128)(2,1)S(1)} %add_convert_fusion.2), channel_id=1, source_target_pairs={{0,8},{1,9},{2,10},{3,11},{4,12},{5,13},{6,14},{7,15},{8,0},{9,1},... | collective-permute-start | bytes 1179656 | tf_op jit(solution)/shard_map/ppermute | solution.py:29
  76.3 83.4 %copy-start.1 = (bf16[32,6144]{1,0:T(8,128)(2,1)}, bf16[32,6144]{1,0:T(8,128)(2,1)S(1)}, u32[]{:S(2)}) copy-start(bf16[32,6144]{1,0:T(8,128)(2,1)S(1)} %get-tuple-element.34) | copy-start | bytes 1179652
  76.3 26.8 %collective-permute-start.17 = (bf16[32,6144]{1,0:T(8,128)(2,1)S(1)}, bf16[32,6144]{1,0:T(8,128)(2,1)S(1)}, u32[]{:S(2)}, u32[]{:S(2)}) collective-permute-start(bf16[32,6144]{1,0:T(8,128)(2,1)S(1)} %get-tuple-element.34), channel_id=1, source_target_pairs={{0,8},{1,9},{2,10},{3,11},{4,12},{5,13},{6,14},{7,15},{8,0},{9,1},... | collective-permute-start | bytes 1179656 | tf_op jit(solution)/shard_map/ppermute | solution.py:29
  81.6 78.9 %collective-permute-start.24 = (bf16[384,6144]{1,0:T(8,128)(2,1)}, bf16[384,6144]{1,0:T(8,128)(2,1)}, u32[]{:S(2)}, u32[]{:S(2)}) collective-permute-start(bf16[384,6144]{1,0:T(8,128)(2,1)} %w_ref.3), channel_id=1, source_target_pairs={{0,1},{1,0},{2,3},{3,2},{4,5},{5,4},{6,7},{7,6},{8,9},{9,8},{10,11... | collective-permute-start | bytes 14155784 | tf_op jit(solution)/shard_map/ppermute | solution.py:25
  103.2 27.1 %collective-permute-start.18 = (bf16[32,6144]{1,0:T(8,128)(2,1)S(1)}, bf16[32,6144]{1,0:T(8,128)(2,1)S(1)}, u32[]{:S(2)}, u32[]{:S(2)}) collective-permute-start(bf16[32,6144]{1,0:T(8,128)(2,1)S(1)} %collective-permute-done.17), channel_id=1, source_target_pairs={{0,6},{1,7},{2,0},{3,1},{4,2},{5,3},{6,4},{7,5},{8,14},{9,15},{10,... | collective-permute-start | bytes 1179656 | tf_op jit(solution)/shard_map/ppermute | solution.py:33
  107.5 43.8 %collective-permute-start.21 = (bf16[32,6144]{1,0:T(8,128)(2,1)S(1)}, bf16[32,6144]{1,0:T(8,128)(2,1)S(1)}, u32[]{:S(2)}, u32[]{:S(2)}) collective-permute-start(bf16[32,6144]{1,0:T(8,128)(2,1)S(1)} %get-tuple-element.34), channel_id=1, source_target_pairs={{0,6},{1,7},{2,0},{3,1},{4,2},{5,3},{6,4},{7,5},{8,14},{9,15},{10,... | collective-permute-start | bytes 1179656 | tf_op jit(solution)/shard_map/ppermute | solution.py:33
  107.8 47.2 %collective-permute-start.22 = (bf16[32,6144]{1,0:T(8,128)(2,1)S(1)}, bf16[32,6144]{1,0:T(8,128)(2,1)S(1)}, u32[]{:S(2)}, u32[]{:S(2)}) collective-permute-start(bf16[32,6144]{1,0:T(8,128)(2,1)S(1)} %get-tuple-element.34), channel_id=1, source_target_pairs={{0,4},{1,5},{2,6},{3,7},{4,0},{5,1},{6,2},{7,3},{8,12},{9,13},{10,... | collective-permute-start | bytes 1179656 | tf_op jit(solution)/shard_map/ppermute | solution.py:33
  107.9 47.9 %collective-permute-start.23 = (bf16[32,6144]{1,0:T(8,128)(2,1)S(1)}, bf16[32,6144]{1,0:T(8,128)(2,1)S(1)}, u32[]{:S(2)}, u32[]{:S(2)}) collective-permute-start(bf16[32,6144]{1,0:T(8,128)(2,1)S(1)} %get-tuple-element.34), channel_id=1, source_target_pairs={{0,2},{1,3},{2,4},{3,5},{4,6},{5,7},{6,0},{7,1},{8,10},{9,11},{10,... | collective-permute-start | bytes 1179656 | tf_op jit(solution)/shard_map/ppermute | solution.py:33
  110.0 32.3 %all-to-all-start = ((bf16[16,32,384]{2,1,0:T(8,128)(2,1)}), bf16[16,32,384]{2,1,0:T(8,128)(2,1)S(1)}, u32[]{:S(2)}, u32[]{:S(2)}) async-start(bf16[16,32,384]{2,1,0:T(8,128)(2,1)} %bitcast.69), calls=%async_computation | async-start | bytes 786432 | tf_op jit(solution)/shard_map/all_to_all | solution.py:127
  130.3 10.6 %collective-permute-start.19 = (bf16[32,6144]{1,0:T(8,128)(2,1)S(1)}, bf16[32,6144]{1,0:T(8,128)(2,1)S(1)}, u32[]{:S(2)}, u32[]{:S(2)}) collective-permute-start(bf16[32,6144]{1,0:T(8,128)(2,1)S(1)} %collective-permute-done.17), channel_id=1, source_target_pairs={{0,4},{1,5},{2,6},{3,7},{4,0},{5,1},{6,2},{7,3},{8,12},{9,13},{10,... | collective-permute-start | bytes 1179656 | tf_op jit(solution)/shard_map/ppermute | solution.py:33
  140.9 8.7 %collective-permute-start.20 = (bf16[32,6144]{1,0:T(8,128)(2,1)S(1)}, bf16[32,6144]{1,0:T(8,128)(2,1)S(1)}, u32[]{:S(2)}, u32[]{:S(2)}) collective-permute-start(bf16[32,6144]{1,0:T(8,128)(2,1)S(1)} %collective-permute-done.17), channel_id=1, source_target_pairs={{0,2},{1,3},{2,4},{3,5},{4,6},{5,7},{6,0},{7,1},{8,10},{9,11},{10,... | collective-permute-start | bytes 1179656 | tf_op jit(solution)/shard_map/ppermute | solution.py:33
  149.6 28.3 %collective-permute-start.14 = (bf16[512,384]{1,0:T(8,128)(2,1)S(1)}, bf16[512,384]{1,0:T(8,128)(2,1)S(1)}, u32[]{:S(2)}, u32[]{:S(2)}) collective-permute-start(bf16[512,384]{1,0:T(8,128)(2,1)S(1)} %bitcast.75), channel_id=1, source_target_pairs={{0,6},{1,7},{2,0},{3,1},{4,2},{5,3},{6,4},{7,5},{8,14},{9,15},{10,... | collective-permute-start | bytes 1179656 | tf_op jit(solution)/shard_map/ppermute | solution.py:33
  151.3 27.2 %collective-permute-start.15 = (bf16[512,384]{1,0:T(8,128)(2,1)S(1)}, bf16[512,384]{1,0:T(8,128)(2,1)S(1)}, u32[]{:S(2)}, u32[]{:S(2)}) collective-permute-start(bf16[512,384]{1,0:T(8,128)(2,1)S(1)} %bitcast.76), channel_id=1, source_target_pairs={{0,4},{1,5},{2,6},{3,7},{4,0},{5,1},{6,2},{7,3},{8,12},{9,13},{10,... | collective-permute-start | bytes 1179656 | tf_op jit(solution)/shard_map/ppermute | solution.py:33
  155.0 24.0 %collective-permute-start.16 = (bf16[512,384]{1,0:T(8,128)(2,1)S(1)}, bf16[512,384]{1,0:T(8,128)(2,1)S(1)}, u32[]{:S(2)}, u32[]{:S(2)}) collective-permute-start(bf16[512,384]{1,0:T(8,128)(2,1)S(1)} %bitcast.77), channel_id=1, source_target_pairs={{0,2},{1,3},{2,4},{3,5},{4,6},{5,7},{6,0},{7,1},{8,10},{9,11},{10,... | collective-permute-start | bytes 1179656 | tf_op jit(solution)/shard_map/ppermute | solution.py:33
  155.7 20.6 %collective-permute-start.9 = (bf16[512,384]{1,0:T(8,128)(2,1)S(1)}, bf16[512,384]{1,0:T(8,128)(2,1)S(1)}, u32[]{:S(2)}, u32[]{:S(2)}) collective-permute-start(bf16[512,384]{1,0:T(8,128)(2,1)S(1)} %bitcast.78), channel_id=1, source_target_pairs={{0,8},{1,9},{2,10},{3,11},{4,12},{5,13},{6,14},{7,15},{8,0},{9,1},... | collective-permute-start | bytes 1179656 | tf_op jit(solution)/shard_map/ppermute | solution.py:29
  165.7 13.5 %collective-permute-start.25 = (bf16[256,384]{1,0:T(8,128)(2,1)S(1)}, bf16[256,384]{1,0:T(8,128)(2,1)S(1)}, u32[]{:S(2)}, u32[]{:S(2)}) collective-permute-start(bf16[256,384]{1,0:T(8,128)(2,1)S(1)} %convolution_convert_fusion.1), channel_id=1, source_target_pairs={{0,1},{1,0},{2,3},{3,2},{4,5},{5,4},{6,7},{7,6},{8,9},{9,8},{10,11... | collective-permute-start | bytes 589832 | tf_op jit(solution)/shard_map/ppermute | solution.py:25
  176.3 9.9 %collective-permute-start.10 = (bf16[512,384]{1,0:T(8,128)(2,1)S(1)}, bf16[512,384]{1,0:T(8,128)(2,1)}, u32[]{:S(2)}, u32[]{:S(2)}) collective-permute-start(bf16[512,384]{1,0:T(8,128)(2,1)S(1)} %collective-permute-done.9), channel_id=1, source_target_pairs={{0,6},{1,7},{2,0},{3,1},{4,2},{5,3},{6,4},{7,5},{8,14},{9,15},{10,... | collective-permute-start | bytes 1179656 | tf_op jit(solution)/shard_map/ppermute | solution.py:33
  177.9 9.7 %collective-permute-start.11 = (bf16[512,384]{1,0:T(8,128)(2,1)S(1)}, bf16[512,384]{1,0:T(8,128)(2,1)}, u32[]{:S(2)}, u32[]{:S(2)}) collective-permute-start(bf16[512,384]{1,0:T(8,128)(2,1)S(1)} %collective-permute-done.9), channel_id=1, source_target_pairs={{0,4},{1,5},{2,6},{3,7},{4,0},{5,1},{6,2},{7,3},{8,12},{9,13},{10,... | collective-permute-start | bytes 1179656 | tf_op jit(solution)/shard_map/ppermute | solution.py:33
  178.5 20.5 %collective-permute-start.12 = (bf16[512,384]{1,0:T(8,128)(2,1)S(1)}, bf16[512,384]{1,0:T(8,128)(2,1)}, u32[]{:S(2)}, u32[]{:S(2)}) collective-permute-start(bf16[512,384]{1,0:T(8,128)(2,1)S(1)} %collective-permute-done.9), channel_id=1, source_target_pairs={{0,2},{1,3},{2,4},{3,5},{4,6},{5,7},{6,0},{7,1},{8,10},{9,11},{10,... | collective-permute-start | bytes 1179656 | tf_op jit(solution)/shard_map/ppermute | solution.py:33
  221.7 10.0 %collective-permute-start.26 = (f32[384,384]{1,0:T(8,128)S(1)}, f32[384,384]{1,0:T(8,128)S(1)}, u32[]{:S(2)}, u32[]{:S(2)}) collective-permute-start(f32[384,384]{1,0:T(8,128)S(1)} %slice.91), channel_id=1, source_target_pairs={{0,1},{1,0},{2,3},{3,2},{4,5},{5,4},{6,7},{7,6},{8,9},{9,8},{10,11... | collective-permute-start | bytes 1769480 | tf_op jit(solution)/shard_map/ppermute | solution.py:25
  (4 other events, 83.3 us)
Sparse Core Ops, SparseCore 0:
  30.2 91.9 all-gather.2
  124.0 93.7 all-gather.4
where the time goes:
time: 240 us; the launch traced here: 239 us
  waiting for transfers between devices  97 us (40%)
  starting transfers between devices  76.9 us (32%)
  matrix products  17.7 us (7%)
  between operations  14.4 us (6%)
  Pallas kernels  13.2 us (6%)
  local copies, waits for them, and re-layouts  11 us (5%)
  other arithmetic  9.29 us (4%)
    ppermute x18, waiting for transfers between devices, to_x(): return lax.ppermute(a, 'mp', mp_perm(dx=dx))  53.9 us
    ppermute x6, starting transfers between devices, to_core(): return lax.ppermute(a, 'mp', mp_perm(dc=1))  21.9 us
    ppermute x3, waiting for transfers between devices, to_z(): return lax.ppermute(a, 'mp', mp_perm(dz=1))  21.4 us
    ppermute x18, starting transfers between devices, to_x(): return lax.ppermute(a, 'mp', mp_perm(dx=dx))  20.5 us
    all_to_all x1, starting transfers between devices, per_device(): turned = lax.all_to_all(blocks, 'dp', 0, 0, tiled=True)  20.3 us
    all_gather x1, waiting for transfers between devices, per_device(): lax.all_gather(jnp.concatenate([ctx[1], there[:quarter]], axis=1), 'dp',...  17.3 us
    ppermute x3, starting transfers between devices, to_z(): return lax.ppermute(a, 'mp', mp_perm(dz=1))  14.1 us
    pallas_call x2, Pallas kernels, project(): pl.pallas_call(project_kernel, grid=(features // tile,), in_specs=[pl.Blo...  13.2 us
  transfers between devices with their start and end apart: 30, of which 16 were waited for; matrix products, arithmetic and copies ran while one was open for 13% of the time, Pallas kernels for 3%

commit v1 on v0

--- a/solution.py
+++ b/solution.py
@@ -65,10 +65,14 @@
     )(a, w)
 
 
-def reduce_x(q):
+def send_x(q):
     r = q.shape[0] // 4
     b1, b2, b3, b0 = (q[i * r : (i + 1) * r] for i in range(4))
-    return add(b0, to_x(b1, 1), to_x(b2, 2), to_x(b3, 3))
+    return [b0, to_x(b1, 1), to_x(b2, 2), to_x(b3, 3)]
+
+
+def after(*values):
+    return lax.optimization_barrier(values)
 
 
 def gather_x(b):
@@ -99,16 +103,21 @@
     ctx = context.reshape(16, r, width)[idx].reshape(4, quarter, width)
 
     other0, own0 = project(ctx[:2].reshape(2 * quarter, width), w_out)
-    q0 = add(own0, to_core(other0)).astype(BF16)
-    other1, own1 = project(ctx[2:].reshape(2 * quarter, width), w_out)
+    there = to_core(ctx[::2].reshape(2 * quarter, width))
+    from0 = to_core(other0)
+    ctx_low, from0, there = after(ctx[2:], from0, there)
+    sent0 = send_x(add(own0, from0).astype(BF16))
+    other1, own1 = project(ctx_low.reshape(2 * quarter, width), w_out)
     q1 = add(own1, to_core(other1)).astype(BF16)
-    z0 = to_z(reduce_x(q0).astype(BF16))
-    mixed = reduce_x(q1)
+    q1, *sent0 = after(q1, *sent0)
+    z0 = to_z(add(*sent0).astype(BF16))
+    sent1 = send_x(q1)
 
-    there = to_core(ctx[::2].reshape(2 * quarter, width))
-    ctx_far = lax.all_gather(jnp.concatenate([ctx[1], there[:quarter]], axis=1), "dp", axis=0, tiled=True)
-    ctx_near = lax.all_gather(jnp.concatenate([ctx[3], there[quarter:]], axis=1), "dp", axis=0, tiled=True)
+    pair = jnp.concatenate([ctx[1::2].reshape(2 * quarter, width), there], axis=1)
+    ctx_all = lax.all_gather(pair, "dp", axis=0)
     w_sibling = to_core(w_out)
+    z0, w_sibling, *sent1 = after(z0, w_sibling, *sent1)
+    mixed = add(*sent1)
 
     presum = mixed + z0.astype(F32) + residual.astype(F32)
     average = jnp.mean(presum, axis=-1, keepdims=True)
@@ -121,14 +130,19 @@
     second = jnp.mean(scaled * xhat, axis=-1, keepdims=True)
     grad = (inverse * (scaled - first - xhat * second)).astype(BF16)
 
+    far0 = to_z(grad)
     near = gather_x(grad)
-    far = gather_x(to_z(grad))
-    blocks = grad.reshape(r, 16, width).transpose(1, 0, 2).reshape(rows, width)
+    near_g, far0 = after(near, far0)
+    blocks = near_g[3].reshape(r, 16, width).transpose(1, 0, 2).reshape(rows, width)
     turned = lax.all_to_all(blocks, "dp", 0, 0, tiled=True)
+    far = gather_x(far0)
+    turned, far = after(turned, far)
+    turned_far0 = to_z(turned)
     turned_near = gather_x(turned)
-    turned_far = gather_x(to_z(turned))
+    turned_near, turned_far0, ctx_all = after(turned_near, turned_far0, ctx_all)
+    turned_far = gather_x(turned_far0)
 
-    gathered = jnp.concatenate(far + near, axis=0)
+    gathered = jnp.concatenate(far + near_g, axis=0)
     cg_own = contract_columns(gathered, w_out).astype(BF16)
     cg_sibling = contract_columns(gathered, w_sibling).astype(BF16)
     cg = jnp.concatenate([to_core(cg_sibling), cg_own], axis=0)
@@ -137,8 +151,10 @@
     ]
     context_grad = cg.reshape(16, r, width)[jnp.stack(pos)].reshape(rows, width)
 
+    ctx_far = ctx_all[:, :quarter].reshape(16 * quarter, 2 * width)
+    ctx_near = ctx_all[:, quarter:].reshape(16 * quarter, 2 * width)
     wg_near = contract_rows(ctx_near, by_image(turned_near))
-    turned_far, wg_near, context_grad = lax.optimization_barrier((turned_far, wg_near, context_grad))
+    turned_far, wg_near, ctx_far, context_grad = after(turned_far, wg_near, ctx_far, context_grad)
     wg = wg_near + contract_rows(ctx_far, by_image(turned_far))
     weight_grad = (wg[:width] + to_core(wg[width:])) * row_factor
     return (normed, grad, context_grad, weight_grad)

time: 240 us -> 244 us (1.017)
  the two profiles are of different devices: /device:TPU:1 before, /device:TPU:73 now
where the time goes in v1:
time: 244 us; the launch traced here: 243 us
  waiting for transfers between devices  93.8 us (38%)
  starting transfers between devices  82.1 us (34%)
  local copies, waits for them, and re-layouts  19.7 us (8%)
  between operations  14.5 us (6%)
  Pallas kernels  13.2 us (5%)
  matrix products  10.9 us (4%)
  other arithmetic  8.77 us (4%)
    ppermute x18, waiting for transfers between devices, to_x(): return lax.ppermute(a, 'mp', mp_perm(dx=dx))  79.9 us
    all_to_all x1, starting transfers between devices, per_device(): turned = lax.all_to_all(blocks, 'dp', 0, 0, tiled=True)  37.6 us
    ppermute x18, starting transfers between devices, to_x(): return lax.ppermute(a, 'mp', mp_perm(dx=dx))  28.4 us
    pallas_call x2, Pallas kernels, project(): pl.pallas_call(project_kernel, grid=(features // tile,), in_specs=[pl.Blo...  13.2 us
    ppermute x3, starting transfers between devices, to_z(): return lax.ppermute(a, 'mp', mp_perm(dz=1))  10.8 us
    ppermute x3, waiting for transfers between devices, to_z(): return lax.ppermute(a, 'mp', mp_perm(dz=1))  9.75 us
    optimization_barrier x1, local copies, waits for them, and re-layouts, after(): return lax.optimization_barrier(values)  8.67 us
    dot_general x2, matrix products, contract_columns(): lax.dot_general(a, b, (((1,), (1,)), ((), ())), preferred_element_type=F32)  6.1 us
  transfers between devices with their start and end apart: 29, of which 17 were waited for; matrix products, arithmetic and copies ran while one was open for 9% of the time, Pallas kernels for 3%

profile of v1, /device:TPU:73, one launch (start us, length us, event | category | flops | bytes accessed | tf_op | source)
XLA Modules:
  0.0 243.1 jit_solution(4550191556401601040)
XLA Ops:
  9.6 6.6 %shard_map.84 = (bf16[128,6144]{1,0:T(8,128)(2,1)}, bf16[128,6144]{1,0:T(8,128)(2,1)}) custom-call(bf16[256,384]{1,0:T(8,128)(2,1)} %bitcast.83, bf16[384,6144]{1,0:T(8,128)(2,1)} %w_ref.3), custom_call_target="tpu_custom_call" | custom-call | flops 1207959552 | bytes 7864320 | tf_op jit(solution)/shard_map/pallas_call | solution.py:56
  18.1 2.5 %collective-permute-done.1 = bf16[256,384]{1,0:T(8,128)(2,1)} collective-permute-done((bf16[256,384]{1,0:T(8,128)(2,1)S(1)}, bf16[256,384]{1,0:T(8,128)(2,1)}, u32[]{:S(2)}, u32[]{:S(2)}) %collective-permute-start.1) | collective-permute-done | bytes 196640 | tf_op jit(solution)/shard_map/ppermute | solution.py:25
  20.6 6.6 %shard_map.85 = (bf16[128,6144]{1,0:T(8,128)(2,1)}, bf16[128,6144]{1,0:T(8,128)(2,1)}) custom-call(bf16[256,384]{1,0:T(8,128)(2,1)} %bitcast.82, bf16[384,6144]{1,0:T(8,128)(2,1)} %w_ref.3), custom_call_target="tpu_custom_call" | custom-call | flops 1207959552 | bytes 7864320 | tf_op jit(solution)/shard_map/pallas_call | solution.py:56
  27.6 1.8 add_convert_fusion
  31.8 2.5 %collective-permute-start.4 = (bf16[32,6144]{1,0:T(8,128)(2,1)}, bf16[32,6144]{1,0:T(8,128)(2,1)}, u32[]{:S(2)}, u32[]{:S(2)}) collective-permute-start(bf16[32,6144]{1,0:T(8,128)(2,1)} %get-tuple-element.95), channel_id=1, source_target_pairs={{0,4},{1,5},{2,6},{3,7},{4,0},{5,1},{6,2},{7,3},{8,12},{9,13},{10,... | collective-permute-start | bytes 1179656 | tf_op jit(solution)/shard_map/ppermute | solution.py:33
  35.4 1.7 pad_maximum_fusion.1
  37.6 5.1 %collective-permute-done.3 = bf16[32,6144]{1,0:T(8,128)(2,1)} collective-permute-done((bf16[32,6144]{1,0:T(8,128)(2,1)}, bf16[32,6144]{1,0:T(8,128)(2,1)}, u32[]{:S(2)}, u32[]{:S(2)}) %collective-permute-start.3) | collective-permute-done | bytes 393248 | tf_op jit(solution)/shard_map/ppermute | solution.py:33
  42.7 9.4 %collective-permute-done.4 = bf16[32,6144]{1,0:T(8,128)(2,1)} collective-permute-done((bf16[32,6144]{1,0:T(8,128)(2,1)}, bf16[32,6144]{1,0:T(8,128)(2,1)}, u32[]{:S(2)}, u32[]{:S(2)}) %collective-permute-start.4) | collective-permute-done | bytes 393248 | tf_op jit(solution)/shard_map/ppermute | solution.py:33
  52.2 2.5 %collective-permute-start.10 = (bf16[32,6144]{1,0:T(8,128)(2,1)S(1)}, bf16[32,6144]{1,0:T(8,128)(2,1)S(1)}, u32[]{:S(2)}, u32[]{:S(2)}) collective-permute-start(bf16[32,6144]{1,0:T(8,128)(2,1)S(1)} %get-tuple-element.90), channel_id=1, source_target_pairs={{0,6},{1,7},{2,0},{3,1},{4,2},{5,3},{6,4},{7,5},{8,14},{9,15},{10,... | collective-permute-start | bytes 1179656 | tf_op jit(solution)/shard_map/ppermute | solution.py:33
  57.5 5.2 %collective-permute-start.6 = (bf16[32,6144]{1,0:T(8,128)(2,1)S(1)}, bf16[32,6144]{1,0:T(8,128)(2,1)S(1)}, u32[]{:S(2)}, u32[]{:S(2)}) collective-permute-start(bf16[32,6144]{1,0:T(8,128)(2,1)S(1)} %add_convert_fusion.2), channel_id=1, source_target_pairs={{0,8},{1,9},{2,10},{3,11},{4,12},{5,13},{6,14},{7,15},{8,0},{9,1},... | collective-permute-start | bytes 1179656 | tf_op jit(solution)/shard_map/ppermute | solution.py:29
  64.0 10.2 %collective-permute-done.8 = bf16[32,6144]{1,0:T(8,128)(2,1)S(1)} collective-permute-done((bf16[32,6144]{1,0:T(8,128)(2,1)S(1)}, bf16[32,6144]{1,0:T(8,128)(2,1)S(1)}, u32[]{:S(2)}, u32[]{:S(2)}) %collective-permute-start.8) | collective-permute-done | bytes 393248 | tf_op jit(solution)/shard_map/ppermute | solution.py:33
  74.3 6.0 %collective-permute-done.6 = bf16[32,6144]{1,0:T(8,128)(2,1)S(1)} collective-permute-done((bf16[32,6144]{1,0:T(8,128)(2,1)S(1)}, bf16[32,6144]{1,0:T(8,128)(2,1)S(1)}, u32[]{:S(2)}, u32[]{:S(2)}) %collective-permute-start.6) | collective-permute-done | bytes 393248 | tf_op jit(solution)/shard_map/ppermute | solution.py:29
  83.8 2.3 collective-permute-start.12
  86.2 4.7 %collective-permute-start.14 = (bf16[32,6144]{1,0:T(8,128)(2,1)S(1)}, bf16[32,6144]{1,0:T(8,128)(2,1)S(1)}, u32[]{:S(2)}, u32[]{:S(2)}) collective-permute-start(bf16[32,6144]{1,0:T(8,128)(2,1)S(1)} %get-tuple-element.61), channel_id=1, source_target_pairs={{0,8},{1,9},{2,10},{3,11},{4,12},{5,13},{6,14},{7,15},{8,0},{9,1},... | collective-permute-start | bytes 1179656 | tf_op jit(solution)/shard_map/ppermute | solution.py:29
  92.5 1.8 collective-permute-done.12
  94.3 10.4 %collective-permute-done.13 = bf16[32,6144]{1,0:T(8,128)(2,1)S(1)} collective-permute-done((bf16[32,6144]{1,0:T(8,128)(2,1)S(1)}, bf16[32,6144]{1,0:T(8,128)(2,1)S(1)}, u32[]{:S(2)}, u32[]{:S(2)}) %collective-permute-start.13) | collective-permute-done | bytes 393248 | tf_op jit(solution)/shard_map/ppermute | solution.py:33
  105.6 37.6 %all-to-all-start = ((bf16[16,32,384]{2,1,0:T(8,128)(2,1)}), bf16[16,32,384]{2,1,0:T(8,128)(2,1)S(1)}, u32[]{:S(2)}, u32[]{:S(2)}) async-start(bf16[16,32,384]{2,1,0:T(8,128)(2,1)} %bitcast.71), calls=%async_computation | async-start | bytes 786432 | tf_op jit(solution)/shard_map/all_to_all | solution.py:137
  144.1 9.1 %collective-permute-start.16 = (bf16[32,6144]{1,0:T(8,128)(2,1)S(1)}, bf16[32,6144]{1,0:T(8,128)(2,1)S(1)}, u32[]{:S(2)}, u32[]{:S(2)}) collective-permute-start(bf16[32,6144]{1,0:T(8,128)(2,1)S(1)} %collective-permute-done.14), channel_id=1, source_target_pairs={{0,4},{1,5},{2,6},{3,7},{4,0},{5,1},{6,2},{7,3},{8,12},{9,13},{10,... | collective-permute-start | bytes 1179656 | tf_op jit(solution)/shard_map/ppermute | solution.py:33
  153.3 6.4 %collective-permute-done.15 = bf16[32,6144]{1,0:T(8,128)(2,1)S(1)} collective-permute-done((bf16[32,6144]{1,0:T(8,128)(2,1)S(1)}, bf16[32,6144]{1,0:T(8,128)(2,1)S(1)}, u32[]{:S(2)}, u32[]{:S(2)}) %collective-permute-start.15) | collective-permute-done | bytes 393248 | tf_op jit(solution)/shard_map/ppermute | solution.py:33
  161.2 10.1 %collective-permute-done.17 = bf16[32,6144]{1,0:T(8,128)(2,1)} collective-permute-done((bf16[32,6144]{1,0:T(8,128)(2,1)S(1)}, bf16[32,6144]{1,0:T(8,128)(2,1)}, u32[]{:S(2)}, u32[]{:S(2)}) %collective-permute-start.17) | collective-permute-done | bytes 393248 | tf_op jit(solution)/shard_map/ppermute | solution.py:33
  175.9 4.3 %convolution_convert_fusion.1 = bf16[256,384]{1,0:T(8,128)(2,1)S(1)} fusion(bf16[256,6144]{1,0:T(8,128)(2,1)S(1)} %constant_dynamic-update-slice_fusion, bf16[384,6144]{1,0:T(8,128)(2,1)} %collective-permute-done.7), kind=kOutput, calls=%fused_computation.16 | convolution fusion | flops 1208057856 | bytes 8060928 | tf_op jit(solution)/shard_map/dot_general | solution.py:87
  180.2 3.2 %collective-permute-start.25 = (bf16[256,384]{1,0:T(8,128)(2,1)S(1)}, bf16[256,384]{1,0:T(8,128)(2,1)S(1)}, u32[]{:S(2)}, u32[]{:S(2)}) collective-permute-start(bf16[256,384]{1,0:T(8,128)(2,1)S(1)} %convolution_convert_fusion.1), channel_id=1, source_target_pairs={{0,1},{1,0},{2,3},{3,2},{4,5},{5,4},{6,7},{7,6},{8,9},{9,8},{10,11... | collective-permute-start | bytes 589832 | tf_op jit(solution)/shard_map/ppermute | solution.py:25
  183.4 1.8 convolution_convert_fusion
  186.6 5.7 %collective-permute-done.20 = bf16[512,384]{1,0:T(8,128)(2,1)} collective-permute-done((bf16[512,384]{1,0:T(8,128)(2,1)S(1)}, bf16[512,384]{1,0:T(8,128)(2,1)}, u32[]{:S(2)}, u32[]{:S(2)}) %collective-permute-start.20) | collective-permute-done | bytes 393248 | tf_op jit(solution)/shard_map/ppermute | solution.py:33
  192.4 3.8 %collective-permute-done.21 = bf16[512,384]{1,0:T(8,128)(2,1)S(1)} collective-permute-done((bf16[512,384]{1,0:T(8,128)(2,1)S(1)}, bf16[512,384]{1,0:T(8,128)(2,1)S(1)}, u32[]{:S(2)}, u32[]{:S(2)}) %collective-permute-start.21) | collective-permute-done | bytes 393248 | tf_op jit(solution)/shard_map/ppermute | solution.py:29
  196.2 8.7 %copy.10 = bf16[16,256,768]{1,2,0:T(8,128)(2,1)} copy(bf16[16,256,768]{2,1,0:T(8,128)(2,1)} %bitcast.75) | data formatting | bytes 12582912 | tf_op jit(solution)/shard_map/optimization_barrier | solution.py:75
  204.8 2.3 slice.66
  207.2 2.8 %collective-permute-start.22 = (bf16[512,384]{1,0:T(8,128)(2,1)S(1)}, bf16[512,384]{1,0:T(8,128)(2,1)S(1)}, u32[]{:S(2)}, u32[]{:S(2)}) collective-permute-start(bf16[512,384]{1,0:T(8,128)(2,1)S(1)} %collective-permute-done.21), channel_id=1, source_target_pairs={{0,6},{1,7},{2,0},{3,1},{4,2},{5,3},{6,4},{7,5},{8,14},{9,15},{10,... | collective-permute-start | bytes 1179656 | tf_op jit(solution)/shard_map/ppermute | solution.py:33
  211.7 3.0 %fusion.9 = f32[768,384]{1,0:T(8,128)S(1)} fusion(bf16[16,32,384]{2,1,0:T(8,128)(2,1)S(1)} %all-to-all-done, bf16[16,32,384]{2,1,0:T(8,128)(2,1)} %bitcast.29, bf16[16,32,384]{2,1,0:T(8,128)(2,1)} %bitcast.28, bf16[16,32,384]{2,1,0:T(8,128)(2,1)} %bitcast.27, bf16[16,256,768]{1,2,0:T(8,128)(2,1)S(1)} %copy-done.1), kind=kOutput, calls=%fused_computation.14 | convolution fusion | flops 1214251008 | bytes 5898240 | tf_op jit(solution)/shard_map/dot_general | solution.py:83
  214.7 11.5 %collective-permute-done.22 = bf16[512,384]{1,0:T(8,128)(2,1)S(1)} collective-permute-done((bf16[512,384]{1,0:T(8,128)(2,1)S(1)}, bf16[512,384]{1,0:T(8,128)(2,1)S(1)}, u32[]{:S(2)}, u32[]{:S(2)}) %collective-permute-start.22) | collective-permute-done | bytes 393248 | tf_op jit(solution)/shard_map/ppermute | solution.py:33
  226.2 4.7 %collective-permute-done.24 = bf16[512,384]{1,0:T(8,128)(2,1)S(1)} collective-permute-done((bf16[512,384]{1,0:T(8,128)(2,1)S(1)}, bf16[512,384]{1,0:T(8,128)(2,1)S(1)}, u32[]{:S(2)}, u32[]{:S(2)}) %collective-permute-start.24) | collective-permute-done | bytes 393248 | tf_op jit(solution)/shard_map/ppermute | solution.py:33
  231.1 1.8 fusion.24
  (99 shorter events, 32.5 us)
Async XLA Ops:
  7.2 189.0 %all-gather.3.cloned.1.call-start = ((), (), s32[]{:S(2)}) async-start(), calls=%async_computation.1 | async-start | bytes 6684672 | tf_op jit(solution)/shard_map/all_gather | solution.py:117
  16.2 4.4 %collective-permute-start = (bf16[128,6144]{1,0:T(8,128)(2,1)}, bf16[128,6144]{1,0:T(8,128)(2,1)}, u32[]{:S(2)}, u32[]{:S(2)}) collective-permute-start(bf16[128,6144]{1,0:T(8,128)(2,1)} %get-tuple-element.45), channel_id=1, source_target_pairs={{0,1},{1,0},{2,3},{3,2},{4,5},{5,4},{6,7},{7,6},{8,9},{9,8},{10,11... | collective-permute-start | bytes 4718600 | tf_op jit(solution)/shard_map/ppermute | solution.py:25
  17.6 3.0 %collective-permute-start.1 = (bf16[256,384]{1,0:T(8,128)(2,1)S(1)}, bf16[256,384]{1,0:T(8,128)(2,1)}, u32[]{:S(2)}, u32[]{:S(2)}) collective-permute-start(bf16[256,384]{1,0:T(8,128)(2,1)S(1)} %bitcast.94), channel_id=1, source_target_pairs={{0,1},{1,0},{2,3},{3,2},{4,5},{5,4},{6,7},{7,6},{8,9},{9,8},{10,11... | collective-permute-start | bytes 589832 | tf_op jit(solution)/shard_map/ppermute | solution.py:25
  17.6 62.6 %collective-permute-start.7 = (bf16[384,6144]{1,0:T(8,128)(2,1)}, bf16[384,6144]{1,0:T(8,128)(2,1)}, u32[]{:S(2)}, u32[]{:S(2)}) collective-permute-start(bf16[384,6144]{1,0:T(8,128)(2,1)} %w_ref.3), channel_id=1, source_target_pairs={{0,1},{1,0},{2,3},{3,2},{4,5},{5,4},{6,7},{7,6},{8,9},{9,8},{10,11... | collective-permute-start | bytes 14155784 | tf_op jit(solution)/shard_map/ppermute | solution.py:25
  27.2 9.9 %collective-permute-start.2 = (bf16[128,6144]{1,0:T(8,128)(2,1)}, bf16[128,6144]{1,0:T(8,128)(2,1)S(1)}, u32[]{:S(2)}, u32[]{:S(2)}) collective-permute-start(bf16[128,6144]{1,0:T(8,128)(2,1)} %get-tuple-element.48), channel_id=1, source_target_pairs={{0,1},{1,0},{2,3},{3,2},{4,5},{5,4},{6,7},{7,6},{8,9},{9,8},{10,11... | collective-permute-start | bytes 4718600 | tf_op jit(solution)/shard_map/ppermute | solution.py:25
  30.6 12.1 %collective-permute-start.3 = (bf16[32,6144]{1,0:T(8,128)(2,1)}, bf16[32,6144]{1,0:T(8,128)(2,1)}, u32[]{:S(2)}, u32[]{:S(2)}) collective-permute-start(bf16[32,6144]{1,0:T(8,128)(2,1)} %get-tuple-element.96), channel_id=1, source_target_pairs={{0,2},{1,3},{2,4},{3,5},{4,6},{5,7},{6,0},{7,1},{8,10},{9,11},{10,... | collective-permute-start | bytes 1179656 | tf_op jit(solution)/shard_map/ppermute | solution.py:33
  31.8 20.3 %collective-permute-start.4 = (bf16[32,6144]{1,0:T(8,128)(2,1)}, bf16[32,6144]{1,0:T(8,128)(2,1)}, u32[]{:S(2)}, u32[]{:S(2)}) collective-permute-start(bf16[32,6144]{1,0:T(8,128)(2,1)} %get-tuple-element.95), channel_id=1, source_target_pairs={{0,4},{1,5},{2,6},{3,7},{4,0},{5,1},{6,2},{7,3},{8,12},{9,13},{10,... | collective-permute-start | bytes 1179656 | tf_op jit(solution)/shard_map/ppermute | solution.py:33
  34.3 17.9 %collective-permute-start.5 = (bf16[32,6144]{1,0:T(8,128)(2,1)}, bf16[32,6144]{1,0:T(8,128)(2,1)}, u32[]{:S(2)}, u32[]{:S(2)}) collective-permute-start(bf16[32,6144]{1,0:T(8,128)(2,1)} %get-tuple-element.94), channel_id=1, source_target_pairs={{0,6},{1,7},{2,0},{3,1},{4,2},{5,3},{6,4},{7,5},{8,14},{9,15},{10,... | collective-permute-start | bytes 1179656 | tf_op jit(solution)/shard_map/ppermute | solution.py:33
  37.6 42.7 %copy-start.9 = (bf16[32,6144]{1,0:T(8,128)(2,1)S(1)}, bf16[32,6144]{1,0:T(8,128)(2,1)}, u32[]{:S(2)}) copy-start(bf16[32,6144]{1,0:T(8,128)(2,1)} %param.7) | copy-start | bytes 1179652
  52.2 28.7 %copy-start.5 = (bf16[32,6144]{1,0:T(8,128)(2,1)S(1)}, bf16[32,6144]{1,0:T(8,128)(2,1)}, u32[]{:S(2)}) copy-start(bf16[32,6144]{1,0:T(8,128)(2,1)} %param.9) | copy-start | bytes 1179652
  52.2 11.8 %collective-permute-start.10 = (bf16[32,6144]{1,0:T(8,128)(2,1)S(1)}, bf16[32,6144]{1,0:T(8,128)(2,1)S(1)}, u32[]{:S(2)}, u32[]{:S(2)}) collective-permute-start(bf16[32,6144]{1,0:T(8,128)(2,1)S(1)} %get-tuple-element.90), channel_id=1, source_target_pairs={{0,6},{1,7},{2,0},{3,1},{4,2},{5,3},{6,4},{7,5},{8,14},{9,15},{10,... | collective-permute-start | bytes 1179656 | tf_op jit(solution)/shard_map/ppermute | solution.py:33
  54.8 19.5 %collective-permute-start.8 = (bf16[32,6144]{1,0:T(8,128)(2,1)S(1)}, bf16[32,6144]{1,0:T(8,128)(2,1)S(1)}, u32[]{:S(2)}, u32[]{:S(2)}) collective-permute-start(bf16[32,6144]{1,0:T(8,128)(2,1)S(1)} %get-tuple-element.92), channel_id=1, source_target_pairs={{0,2},{1,3},{2,4},{3,5},{4,6},{5,7},{6,0},{7,1},{8,10},{9,11},{10,... | collective-permute-start | bytes 1179656 | tf_op jit(solution)/shard_map/ppermute | solution.py:33
  54.8 19.5 %collective-permute-start.9 = (bf16[32,6144]{1,0:T(8,128)(2,1)S(1)}, bf16[32,6144]{1,0:T(8,128)(2,1)S(1)}, u32[]{:S(2)}, u32[]{:S(2)}) collective-permute-start(bf16[32,6144]{1,0:T(8,128)(2,1)S(1)} %get-tuple-element.91), channel_id=1, source_target_pairs={{0,4},{1,5},{2,6},{3,7},{4,0},{5,1},{6,2},{7,3},{8,12},{9,13},{10,... | collective-permute-start | bytes 1179656 | tf_op jit(solution)/shard_map/ppermute | solution.py:33
  57.5 22.8 %collective-permute-start.6 = (bf16[32,6144]{1,0:T(8,128)(2,1)S(1)}, bf16[32,6144]{1,0:T(8,128)(2,1)S(1)}, u32[]{:S(2)}, u32[]{:S(2)}) collective-permute-start(bf16[32,6144]{1,0:T(8,128)(2,1)S(1)} %add_convert_fusion.2), channel_id=1, source_target_pairs={{0,8},{1,9},{2,10},{3,11},{4,12},{5,13},{6,14},{7,15},{8,0},{9,1},... | collective-permute-start | bytes 1179656 | tf_op jit(solution)/shard_map/ppermute | solution.py:29
  82.4 93.5 %copy-start.2 = (bf16[32,6144]{1,0:T(8,128)(2,1)}, bf16[32,6144]{1,0:T(8,128)(2,1)S(1)}, u32[]{:S(2)}) copy-start(bf16[32,6144]{1,0:T(8,128)(2,1)S(1)} %get-tuple-element.61) | copy-start | bytes 1179652
  82.4 10.1 %collective-permute-start.11 = (bf16[32,6144]{1,0:T(8,128)(2,1)S(1)}, bf16[32,6144]{1,0:T(8,128)(2,1)S(1)}, u32[]{:S(2)}, u32[]{:S(2)}) collective-permute-start(bf16[32,6144]{1,0:T(8,128)(2,1)S(1)} %get-tuple-element.61), channel_id=1, source_target_pairs={{0,6},{1,7},{2,0},{3,1},{4,2},{5,3},{6,4},{7,5},{8,14},{9,15},{10,... | collective-permute-start | bytes 1179656 | tf_op jit(solution)/shard_map/ppermute | solution.py:33
  83.8 10.5 %collective-permute-start.12 = (bf16[32,6144]{1,0:T(8,128)(2,1)S(1)}, bf16[32,6144]{1,0:T(8,128)(2,1)S(1)}, u32[]{:S(2)}, u32[]{:S(2)}) collective-permute-start(bf16[32,6144]{1,0:T(8,128)(2,1)S(1)} %get-tuple-element.61), channel_id=1, source_target_pairs={{0,4},{1,5},{2,6},{3,7},{4,0},{5,1},{6,2},{7,3},{8,12},{9,13},{10,... | collective-permute-start | bytes 1179656 | tf_op jit(solution)/shard_map/ppermute | solution.py:33
  86.2 18.6 %collective-permute-start.13 = (bf16[32,6144]{1,0:T(8,128)(2,1)S(1)}, bf16[32,6144]{1,0:T(8,128)(2,1)S(1)}, u32[]{:S(2)}, u32[]{:S(2)}) collective-permute-start(bf16[32,6144]{1,0:T(8,128)(2,1)S(1)} %get-tuple-element.61), channel_id=1, source_target_pairs={{0,2},{1,3},{2,4},{3,5},{4,6},{5,7},{6,0},{7,1},{8,10},{9,11},{10,... | collective-permute-start | bytes 1179656 | tf_op jit(solution)/shard_map/ppermute | solution.py:33
  86.2 18.6 %collective-permute-start.14 = (bf16[32,6144]{1,0:T(8,128)(2,1)S(1)}, bf16[32,6144]{1,0:T(8,128)(2,1)S(1)}, u32[]{:S(2)}, u32[]{:S(2)}) collective-permute-start(bf16[32,6144]{1,0:T(8,128)(2,1)S(1)} %get-tuple-element.61), channel_id=1, source_target_pairs={{0,8},{1,9},{2,10},{3,11},{4,12},{5,13},{6,14},{7,15},{8,0},{9,1},... | collective-permute-start | bytes 1179656 | tf_op jit(solution)/shard_map/ppermute | solution.py:29
  105.6 65.7 %all-to-all-start = ((bf16[16,32,384]{2,1,0:T(8,128)(2,1)}), bf16[16,32,384]{2,1,0:T(8,128)(2,1)S(1)}, u32[]{:S(2)}, u32[]{:S(2)}) async-start(bf16[16,32,384]{2,1,0:T(8,128)(2,1)} %bitcast.71), calls=%async_computation | async-start | bytes 786432 | tf_op jit(solution)/shard_map/all_to_all | solution.py:137
  143.1 16.6 %collective-permute-start.15 = (bf16[32,6144]{1,0:T(8,128)(2,1)S(1)}, bf16[32,6144]{1,0:T(8,128)(2,1)S(1)}, u32[]{:S(2)}, u32[]{:S(2)}) collective-permute-start(bf16[32,6144]{1,0:T(8,128)(2,1)S(1)} %collective-permute-done.14), channel_id=1, source_target_pairs={{0,6},{1,7},{2,0},{3,1},{4,2},{5,3},{6,4},{7,5},{8,14},{9,15},{10,... | collective-permute-start | bytes 1179656 | tf_op jit(solution)/shard_map/ppermute | solution.py:33
  144.1 17.1 %collective-permute-start.16 = (bf16[32,6144]{1,0:T(8,128)(2,1)S(1)}, bf16[32,6144]{1,0:T(8,128)(2,1)S(1)}, u32[]{:S(2)}, u32[]{:S(2)}) collective-permute-start(bf16[32,6144]{1,0:T(8,128)(2,1)S(1)} %collective-permute-done.14), channel_id=1, source_target_pairs={{0,4},{1,5},{2,6},{3,7},{4,0},{5,1},{6,2},{7,3},{8,12},{9,13},{10,... | collective-permute-start | bytes 1179656 | tf_op jit(solution)/shard_map/ppermute | solution.py:33
  153.2 18.1 %collective-permute-start.17 = (bf16[32,6144]{1,0:T(8,128)(2,1)S(1)}, bf16[32,6144]{1,0:T(8,128)(2,1)}, u32[]{:S(2)}, u32[]{:S(2)}) collective-permute-start(bf16[32,6144]{1,0:T(8,128)(2,1)S(1)} %collective-permute-done.14), channel_id=1, source_target_pairs={{0,2},{1,3},{2,4},{3,5},{4,6},{5,7},{6,0},{7,1},{8,10},{9,11},{10,... | collective-permute-start | bytes 1179656 | tf_op jit(solution)/shard_map/ppermute | solution.py:33
  171.3 15.3 %collective-permute-start.18 = (bf16[512,384]{1,0:T(8,128)(2,1)S(1)}, bf16[512,384]{1,0:T(8,128)(2,1)}, u32[]{:S(2)}, u32[]{:S(2)}) collective-permute-start(bf16[512,384]{1,0:T(8,128)(2,1)S(1)} %bitcast.89), channel_id=1, source_target_pairs={{0,6},{1,7},{2,0},{3,1},{4,2},{5,3},{6,4},{7,5},{8,14},{9,15},{10,... | collective-permute-start | bytes 1179656 | tf_op jit(solution)/shard_map/ppermute | solution.py:33
  171.3 15.3 %collective-permute-start.19 = (bf16[512,384]{1,0:T(8,128)(2,1)S(1)}, bf16[512,384]{1,0:T(8,128)(2,1)}, u32[]{:S(2)}, u32[]{:S(2)}) collective-permute-start(bf16[512,384]{1,0:T(8,128)(2,1)S(1)} %bitcast.90), channel_id=1, source_target_pairs={{0,4},{1,5},{2,6},{3,7},{4,0},{5,1},{6,2},{7,3},{8,12},{9,13},{10,... | collective-permute-start | bytes 1179656 | tf_op jit(solution)/shard_map/ppermute | solution.py:33
  172.8 19.6 %collective-permute-start.20 = (bf16[512,384]{1,0:T(8,128)(2,1)S(1)}, bf16[512,384]{1,0:T(8,128)(2,1)}, u32[]{:S(2)}, u32[]{:S(2)}) collective-permute-start(bf16[512,384]{1,0:T(8,128)(2,1)S(1)} %bitcast.91), channel_id=1, source_target_pairs={{0,2},{1,3},{2,4},{3,5},{4,6},{5,7},{6,0},{7,1},{8,10},{9,11},{10,... | collective-permute-start | bytes 1179656 | tf_op jit(solution)/shard_map/ppermute | solution.py:33
  172.8 23.4 %collective-permute-start.21 = (bf16[512,384]{1,0:T(8,128)(2,1)S(1)}, bf16[512,384]{1,0:T(8,128)(2,1)S(1)}, u32[]{:S(2)}, u32[]{:S(2)}) collective-permute-start(bf16[512,384]{1,0:T(8,128)(2,1)S(1)} %bitcast.92), channel_id=1, source_target_pairs={{0,8},{1,9},{2,10},{3,11},{4,12},{5,13},{6,14},{7,15},{8,0},{9,1},... | collective-permute-start | bytes 1179656 | tf_op jit(solution)/shard_map/ppermute | solution.py:29
  180.2 5.0 %collective-permute-start.25 = (bf16[256,384]{1,0:T(8,128)(2,1)S(1)}, bf16[256,384]{1,0:T(8,128)(2,1)S(1)}, u32[]{:S(2)}, u32[]{:S(2)}) collective-permute-start(bf16[256,384]{1,0:T(8,128)(2,1)S(1)} %convolution_convert_fusion.1), channel_id=1, source_target_pairs={{0,1},{1,0},{2,3},{3,2},{4,5},{5,4},{6,7},{7,6},{8,9},{9,8},{10,11... | collective-permute-start | bytes 589832 | tf_op jit(solution)/shard_map/ppermute | solution.py:25
  207.2 19.0 %collective-permute-start.22 = (bf16[512,384]{1,0:T(8,128)(2,1)S(1)}, bf16[512,384]{1,0:T(8,128)(2,1)S(1)}, u32[]{:S(2)}, u32[]{:S(2)}) collective-permute-start(bf16[512,384]{1,0:T(8,128)(2,1)S(1)} %collective-permute-done.21), channel_id=1, source_target_pairs={{0,6},{1,7},{2,0},{3,1},{4,2},{5,3},{6,4},{7,5},{8,14},{9,15},{10,... | collective-permute-start | bytes 1179656 | tf_op jit(solution)/shard_map/ppermute | solution.py:33
  209.9 16.3 %collective-permute-start.23 = (bf16[512,384]{1,0:T(8,128)(2,1)S(1)}, bf16[512,384]{1,0:T(8,128)(2,1)S(1)}, u32[]{:S(2)}, u32[]{:S(2)}) collective-permute-start(bf16[512,384]{1,0:T(8,128)(2,1)S(1)} %collective-permute-done.21), channel_id=1, source_target_pairs={{0,4},{1,5},{2,6},{3,7},{4,0},{5,1},{6,2},{7,3},{8,12},{9,13},{10,... | collective-permute-start | bytes 1179656 | tf_op jit(solution)/shard_map/ppermute | solution.py:33
  210.9 20.0 %collective-permute-start.24 = (bf16[512,384]{1,0:T(8,128)(2,1)S(1)}, bf16[512,384]{1,0:T(8,128)(2,1)S(1)}, u32[]{:S(2)}, u32[]{:S(2)}) collective-permute-start(bf16[512,384]{1,0:T(8,128)(2,1)S(1)} %collective-permute-done.21), channel_id=1, source_target_pairs={{0,2},{1,3},{2,4},{3,5},{4,6},{5,7},{6,0},{7,1},{8,10},{9,11},{10,... | collective-permute-start | bytes 1179656 | tf_op jit(solution)/shard_map/ppermute | solution.py:33
  233.1 2.2 collective-permute-start.26
  (10 other events, 107.6 us)
Sparse Core Ops, SparseCore 0:
  37.3 110.5 all-gather.2

commit v2 on v1

--- a/solution.py
+++ b/solution.py
@@ -12,6 +12,9 @@
 DX = (1, 2, 3, 0)
 ORDER = [(dz, dc, dx) for dz in (1, 0) for dc in (1, 0) for dx in DX]
 
+GROUPS_Y = [[4 * z + y for y in range(4)] for z in range(4)]
+Y_THEN_Z = [[4 * z + y for y in range(4) for z in range(4)]]
+
 
 def mp_perm(dz=0, dx=0, dc=0):
     pairs = []
@@ -21,6 +24,10 @@
     return pairs
 
 
+def dp_swap(dz):
+    return [(d, d ^ (4 * dz)) for d in range(16)]
+
+
 def to_core(a):
     return lax.ppermute(a, "mp", mp_perm(dc=1))
 
@@ -50,7 +57,7 @@
 def project(a, w):
     rows, width = a.shape
     features = w.shape[1]
-    tile = min(1024, features)
+    tile = min(2048, features)
     half = jax.ShapeDtypeStruct((rows // 2, features), BF16)
     out_spec = pl.BlockSpec((rows // 2, tile), lambda i: (0, i))
     return pl.pallas_call(
@@ -59,6 +66,7 @@
         in_specs=[pl.BlockSpec((rows, width), lambda i: (0, 0)), pl.BlockSpec((width, tile), lambda i: (0, i))],
         out_specs=[out_spec, out_spec],
         out_shape=[half, half],
+        compiler_params=pltpu.CompilerParams(vmem_limit_bytes=24 * 2**20),
         cost_estimate=pl.CostEstimate(
             flops=2 * rows * width * features, bytes_accessed=2 * features * (rows + width), transcendentals=0
         ),
@@ -79,12 +87,61 @@
     return [to_x(b, 3), to_x(b, 2), to_x(b, 1), b]
 
 
+def spread_z(v, order):
+    four = jnp.concatenate([v, lax.ppermute(v, "dp", dp_swap(2))])
+    return four[order].reshape(-1, v.shape[-1])
+
+
+def gather_y(v):
+    return lax.all_gather(v, "dp", axis=0, axis_index_groups=GROUPS_Y, tiled=True)
+
+
 def contract_rows(a, b):
     return lax.dot_general(a, b, (((0,), (0,)), ((), ())), preferred_element_type=F32)
 
 
-def contract_columns(a, b):
-    return lax.dot_general(a, b, (((1,), (1,)), ((), ())), preferred_element_type=F32)
+def back_project_kernel(*refs):
+    blocks, (w_ref, v_ref, own_ref, sibling_ref, rows_ref, total_ref) = refs[:-6], refs[-6:]
+    r = blocks[0].shape[0]
+    width = w_ref.shape[0]
+    step = pl.program_id(0)
+
+    @pl.when(step == 0)
+    def _():
+        total_ref[...] = jnp.zeros_like(total_ref)
+
+    for k, b in enumerate(blocks):
+        rows_ref[k * r : (k + 1) * r] = b[...]
+    rows = rows_ref[...]
+    for k, w in enumerate((w_ref, v_ref)):
+        total_ref[k] += lax.dot_general(rows, w[...], (((1,), (1,)), ((), ())), preferred_element_type=F32)
+
+    @pl.when(step == pl.num_programs(0) - 1)
+    def _():
+        own_ref[...] = total_ref[0].astype(BF16)
+        sibling_ref[...] = total_ref[1].astype(BF16)
+
+
+def back_project(blocks, w, v):
+    r, features = blocks[0].shape
+    rows, width = r * len(blocks), w.shape[0]
+    tile = min(2048, features)
+    out = jax.ShapeDtypeStruct((rows, width), BF16)
+    whole = pl.BlockSpec((rows, width), lambda i: (0, 0))
+    block = pl.BlockSpec((r, tile), lambda i: (0, i))
+    weight = pl.BlockSpec((width, tile), lambda i: (0, i))
+    return pl.pallas_call(
+        back_project_kernel,
+        grid=(features // tile,),
+        in_specs=[block] * len(blocks) + [weight, weight],
+        out_specs=[whole, whole],
+        out_shape=[out, out],
+        scratch_shapes=[pltpu.VMEM((rows, tile), BF16), pltpu.VMEM((2, rows, width), F32)],
+        compiler_params=pltpu.CompilerParams(vmem_limit_bytes=24 * 2**20),
+        cost_estimate=pl.CostEstimate(
+            flops=4 * rows * width * features, bytes_accessed=2 * features * (rows + 2 * width), transcendentals=0
+        ),
+    )(*blocks, w, v)
 
 
 def by_image(blocks):
@@ -102,21 +159,24 @@
     idx = jnp.stack([(zh ^ dz) * 8 + ((x + dx) % 4) * 2 + (c ^ dc) for dz, dc, dx in ORDER])
     ctx = context.reshape(16, r, width)[idx].reshape(4, quarter, width)
 
+    there = to_core(ctx[::2])
     other0, own0 = project(ctx[:2].reshape(2 * quarter, width), w_out)
-    there = to_core(ctx[::2].reshape(2 * quarter, width))
+    other0, there = after(other0, there)
     from0 = to_core(other0)
-    ctx_low, from0, there = after(ctx[2:], from0, there)
+    pair = jnp.concatenate([ctx[1::2], there], axis=-1)
+    two = jnp.stack([pair, lax.ppermute(pair, "dp", dp_swap(1))])
+    order_z = (lax.axis_index("dp") // 4) ^ jnp.arange(4)
+    near_z = spread_z(two[:, 1], order_z)
+    ctx_low, from0 = after(ctx[2:], from0)
     sent0 = send_x(add(own0, from0).astype(BF16))
     other1, own1 = project(ctx_low.reshape(2 * quarter, width), w_out)
     q1 = add(own1, to_core(other1)).astype(BF16)
-    q1, *sent0 = after(q1, *sent0)
-    z0 = to_z(add(*sent0).astype(BF16))
+    z0 = add(*sent0).astype(BF16)
+    z0, q1 = after(z0, q1)
+    z0 = to_z(z0)
     sent1 = send_x(q1)
-
-    pair = jnp.concatenate([ctx[1::2].reshape(2 * quarter, width), there], axis=1)
-    ctx_all = lax.all_gather(pair, "dp", axis=0)
-    w_sibling = to_core(w_out)
-    z0, w_sibling, *sent1 = after(z0, w_sibling, *sent1)
+    z0, near_z, *sent1 = after(z0, near_z, *sent1)
+    ctx_near = gather_y(near_z)
     mixed = add(*sent1)
 
     presum = mixed + z0.astype(F32) + residual.astype(F32)
@@ -130,31 +190,31 @@
     second = jnp.mean(scaled * xhat, axis=-1, keepdims=True)
     grad = (inverse * (scaled - first - xhat * second)).astype(BF16)
 
+    grad, w_there = after(grad, w_out)
+    w_sibling = to_core(w_there)
     far0 = to_z(grad)
     near = gather_x(grad)
-    near_g, far0 = after(near, far0)
-    blocks = near_g[3].reshape(r, 16, width).transpose(1, 0, 2).reshape(rows, width)
-    turned = lax.all_to_all(blocks, "dp", 0, 0, tiled=True)
+    far_z = two[:, 0]
+    far0, far_z, w_sibling, *near = after(far0, far_z, w_sibling, *near)
+    blocks = near[3].reshape(r, 4, 4, width).transpose(2, 1, 0, 3).reshape(rows, width)
+    turned = lax.all_to_all(blocks, "dp", 0, 0, axis_index_groups=Y_THEN_Z, tiled=True)
+    far_z = spread_z(far_z, order_z)
     far = gather_x(far0)
-    turned, far = after(turned, far)
+    turned, far_z, *far = after(turned, far_z, *far)
+    ctx_far = gather_y(far_z)
     turned_far0 = to_z(turned)
     turned_near = gather_x(turned)
-    turned_near, turned_far0, ctx_all = after(turned_near, turned_far0, ctx_all)
+    cg_own, cg_sibling = back_project(far + near, w_out, w_sibling)
+    turned_far0, cg_own, cg_sibling, *turned_near = after(turned_far0, cg_own, cg_sibling, *turned_near)
     turned_far = gather_x(turned_far0)
-
-    gathered = jnp.concatenate(far + near_g, axis=0)
-    cg_own = contract_columns(gathered, w_out).astype(BF16)
-    cg_sibling = contract_columns(gathered, w_sibling).astype(BF16)
     cg = jnp.concatenate([to_core(cg_sibling), cg_own], axis=0)
     pos = [
         (1 - ((m % 2) ^ c)) * 8 + (1 - ((m // 8) ^ zh)) * 4 + ((m // 2) % 4 - x + 3) % 4 for m in range(16)
     ]
     context_grad = cg.reshape(16, r, width)[jnp.stack(pos)].reshape(rows, width)
 
-    ctx_far = ctx_all[:, :quarter].reshape(16 * quarter, 2 * width)
-    ctx_near = ctx_all[:, quarter:].reshape(16 * quarter, 2 * width)
     wg_near = contract_rows(ctx_near, by_image(turned_near))
-    turned_far, wg_near, ctx_far, context_grad = after(turned_far, wg_near, ctx_far, context_grad)
+    turned_far, wg_near, context_grad = after(turned_far, wg_near, context_grad)
     wg = wg_near + contract_rows(ctx_far, by_image(turned_far))
     weight_grad = (wg[:width] + to_core(wg[width:])) * row_factor
     return (normed, grad, context_grad, weight_grad)

time: 244 us -> 203 us (0.83)
  the two profiles are of different devices: /device:TPU:73 before, /device:TPU:1 now
where the time goes in v2:
time: 203 us
  waiting for transfers between devices  91.4 us (45%)
  starting transfers between devices  50.6 us (25%)
  between operations  14.6 us (7%)
  local copies, waits for them, and re-layouts  13.8 us (7%)
  other arithmetic  13 us (6%)
  Pallas kernels  11.9 us (6%)
  matrix products  7.46 us (4%)
    ppermute x18, waiting for transfers between devices, to_x(): return lax.ppermute(a, 'mp', mp_perm(dx=dx))  53.6 us
    ppermute x2, waiting for transfers between devices, spread_z(): four = jnp.concatenate([v, lax.ppermute(v, 'dp', dp_swap(2))])  24.1 us
    ppermute x18, starting transfers between devices, to_x(): return lax.ppermute(a, 'mp', mp_perm(dx=dx))  20.4 us
    ppermute x3, starting transfers between devices, to_z(): return lax.ppermute(a, 'mp', mp_perm(dz=1))  11.7 us
    ppermute x3, waiting for transfers between devices, to_z(): return lax.ppermute(a, 'mp', mp_perm(dz=1))  8.72 us
    ppermute x6, starting transfers between devices, to_core(): return lax.ppermute(a, 'mp', mp_perm(dc=1))  7.5 us
    dot_general x2, matrix products, contract_rows(): lax.dot_general(a, b, (((0,), (0,)), ((), ())), preferred_element_type=F32)  7.46 us
    pallas_call x1, Pallas kernels, back_project(): pl.pallas_call(back_project_kernel, grid=(features // tile,), in_specs=[b...  6.63 us
  transfers between devices with their start and end apart: 33, of which 15 were waited for; matrix products, arithmetic and copies ran while one was open for 9% of the time, Pallas kernels for 6%

profile of v2, /device:TPU:1, one launch (start us, length us, event | category | flops | bytes accessed | tf_op | source)
XLA Modules:
  0.0 202.7 jit_solution(295554372958550553)
XLA Ops:
  8.9 3.3 %collective-permute-start = (bf16[2,128,384]{2,1,0:T(8,128)(2,1)S(1)}, bf16[2,128,384]{2,1,0:T(8,128)(2,1)S(1)}, u32[]{:S(2)}, u32[]{:S(2)}) collective-permute-start(bf16[2,128,384]{2,1,0:T(8,128)(2,1)S(1)} %get-tuple-element.114), channel_id=1, source_target_pairs={{0,1},{1,0},{2,3},{3,2},{4,5},{5,4},{6,7},{7,6},{8,9},{9,8},{10,11... | collective-permute-start | bytes 589832 | tf_op jit(solution)/shard_map/ppermute | solution.py:32
  12.2 2.3 %copy-done.1 = bf16[384,6144]{1,0:T(8,128)(2,1)S(1)} copy-done((bf16[384,6144]{1,0:T(8,128)(2,1)S(1)}, bf16[384,6144]{1,0:T(8,128)(2,1)}, u32[]{:S(2)}) %copy-start.1) | copy-done | bytes 4718616
  14.6 2.7 %shard_map.84 = (bf16[128,6144]{1,0:T(8,128)(2,1)S(1)}, bf16[128,6144]{1,0:T(8,128)(2,1)S(1)}) custom-call(bf16[256,384]{1,0:T(8,128)(2,1)S(1)} %bitcast.74, bf16[384,6144]{1,0:T(8,128)(2,1)S(1)} %copy-done.1), custom_call_target="tpu_custom_call" | custom-call | flops 1207959552 | bytes 7864320 | tf_op jit(solution)/shard_map/pallas_call | solution.py:63
  17.5 3.2 %collective-permute-done.1 = bf16[128,6144]{1,0:T(8,128)(2,1)S(1)} collective-permute-done((bf16[128,6144]{1,0:T(8,128)(2,1)S(1)}, bf16[128,6144]{1,0:T(8,128)(2,1)S(1)}, u32[]{:S(2)}, u32[]{:S(2)}) %collective-permute-start.1) | collective-permute-done | bytes 1572896 | tf_op jit(solution)/shard_map/ppermute | solution.py:32
  21.3 1.9 collective-permute-start.3
  24.4 2.7 %shard_map.85 = (bf16[128,6144]{1,0:T(8,128)(2,1)S(1)}, bf16[128,6144]{1,0:T(8,128)(2,1)S(1)}) custom-call(bf16[256,384]{1,0:T(8,128)(2,1)S(1)} %bitcast.73, bf16[384,6144]{1,0:T(8,128)(2,1)S(1)} %copy-done.1), custom_call_target="tpu_custom_call" | custom-call | flops 1207959552 | bytes 7864320 | tf_op jit(solution)/shard_map/pallas_call | solution.py:63
  28.9 3.0 %collective-permute-start.8 = (bf16[2,128,768]{2,1,0:T(8,128)(2,1)S(1)}, bf16[2,128,768]{2,1,0:T(8,128)(2,1)S(1)}, u32[]{:S(2)}, u32[]{:S(2)}) collective-permute-start(bf16[2,128,768]{2,1,0:T(8,128)(2,1)S(1)} %get-tuple-element.110), channel_id=1, source_target_pairs={{0,128},{16,144},{32,160},{48,176},{64,192},{80,208},{96,224},{112... | collective-permute-start | bytes 1179656 | tf_op jit(solution)/shard_map/ppermute | solution.py:91
  31.9 9.6 %collective-permute-done.2 = bf16[32,6144]{1,0:T(8,128)(2,1)S(1)} collective-permute-done((bf16[32,6144]{1,0:T(8,128)(2,1)S(1)}, bf16[32,6144]{1,0:T(8,128)(2,1)S(1)}, u32[]{:S(2)}, u32[]{:S(2)}) %collective-permute-start.2) | collective-permute-done | bytes 393248 | tf_op jit(solution)/shard_map/ppermute | solution.py:40
  44.3 2.5 %collective-permute-start.11 = (bf16[32,6144]{1,0:T(8,128)(2,1)S(1)}, bf16[32,6144]{1,0:T(8,128)(2,1)}, u32[]{:S(2)}, u32[]{:S(2)}) collective-permute-start(bf16[32,6144]{1,0:T(8,128)(2,1)S(1)} %get-tuple-element.100), channel_id=1, source_target_pairs={{0,6},{1,7},{2,0},{3,1},{4,2},{5,3},{6,4},{7,5},{8,14},{9,15},{10,... | collective-permute-start | bytes 1179656 | tf_op jit(solution)/shard_map/ppermute | solution.py:40
  47.0 5.7 %collective-permute-start.6 = (bf16[32,6144]{1,0:T(8,128)(2,1)}, bf16[32,6144]{1,0:T(8,128)(2,1)}, u32[]{:S(2)}, u32[]{:S(2)}) collective-permute-start(bf16[32,6144]{1,0:T(8,128)(2,1)} %add_convert_fusion.2), channel_id=1, source_target_pairs={{0,8},{1,9},{2,10},{3,11},{4,12},{5,13},{6,14},{7,15},{8,0},{9,1},... | collective-permute-start | bytes 1179656 | tf_op jit(solution)/shard_map/ppermute | solution.py:36
  52.8 1.5 gather_fusion.1
  54.3 10.0 %collective-permute-done.11 = bf16[32,6144]{1,0:T(8,128)(2,1)} collective-permute-done((bf16[32,6144]{1,0:T(8,128)(2,1)S(1)}, bf16[32,6144]{1,0:T(8,128)(2,1)}, u32[]{:S(2)}, u32[]{:S(2)}) %collective-permute-start.11) | collective-permute-done | bytes 393248 | tf_op jit(solution)/shard_map/ppermute | solution.py:40
  64.4 1.9 fusion.9
  69.4 5.3 %collective-permute-start.12 = (bf16[32,6144]{1,0:T(8,128)(2,1)S(1)}, bf16[32,6144]{1,0:T(8,128)(2,1)S(1)}, u32[]{:S(2)}, u32[]{:S(2)}) collective-permute-start(bf16[32,6144]{1,0:T(8,128)(2,1)S(1)} %get-tuple-element.67.refs_7_), channel_id=1, source_target_pairs={{0,8},{1,9},{2,10},{3,11},{4,12},{5,13},{6,14},{7,15},{8,0},{9,1},... | collective-permute-start | bytes 1179656 | tf_op jit(solution)/shard_map/ppermute | solution.py:36
  74.6 7.7 %collective-permute-start.14 = (bf16[32,6144]{1,0:T(8,128)(2,1)S(1)}, bf16[32,6144]{1,0:T(8,128)(2,1)S(1)}, u32[]{:S(2)}, u32[]{:S(2)}) collective-permute-start(bf16[32,6144]{1,0:T(8,128)(2,1)S(1)} %get-tuple-element.67.refs_7_), channel_id=1, source_target_pairs={{0,6},{1,7},{2,0},{3,1},{4,2},{5,3},{6,4},{7,5},{8,14},{9,15},{10,... | collective-permute-start | bytes 1179656 | tf_op jit(solution)/shard_map/ppermute | solution.py:40
  84.1 14.8 %collective-permute-done.14.refs_4_ = bf16[32,6144]{1,0:T(8,128)(2,1)S(1)} collective-permute-done((bf16[32,6144]{1,0:T(8,128)(2,1)S(1)}, bf16[32,6144]{1,0:T(8,128)(2,1)S(1)}, u32[]{:S(2)}, u32[]{:S(2)}) %collective-permute-start.14) | collective-permute-done | bytes 393248 | tf_op jit(solution)/shard_map/ppermute | solution.py:40
  98.9 4.6 %collective-permute-done.16.refs_6_ = bf16[32,6144]{1,0:T(8,128)(2,1)S(1)} collective-permute-done((bf16[32,6144]{1,0:T(8,128)(2,1)S(1)}, bf16[32,6144]{1,0:T(8,128)(2,1)S(1)}, u32[]{:S(2)}, u32[]{:S(2)}) %collective-permute-start.16) | collective-permute-done | bytes 393248 | tf_op jit(solution)/shard_map/ppermute | solution.py:40
  104.6 5.5 %all-to-all-start = ((bf16[16,32,384]{2,1,0:T(8,128)(2,1)}), bf16[16,32,384]{2,1,0:T(8,128)(2,1)}, u32[]{:S(2)}, u32[]{:S(2)}) async-start(bf16[16,32,384]{2,1,0:T(8,128)(2,1)} %bitcast.29), calls=%async_computation | async-start | bytes 786432 | tf_op jit(solution)/shard_map/all_to_all | solution.py:200
  110.2 2.3 %collective-permute-start.17 = (bf16[2,128,768]{2,1,0:T(8,128)(2,1)}, bf16[2,128,768]{2,1,0:T(8,128)(2,1)S(1)}, u32[]{:S(2)}, u32[]{:S(2)}) collective-permute-start(bf16[2,128,768]{2,1,0:T(8,128)(2,1)} %get-tuple-element.68), channel_id=1, source_target_pairs={{0,128},{16,144},{32,160},{48,176},{64,192},{80,208},{96,224},{112... | collective-permute-start | bytes 1179656 | tf_op jit(solution)/shard_map/ppermute | solution.py:91
  113.9 24.1 %collective-permute-done.17 = bf16[2,128,768]{2,1,0:T(8,128)(2,1)S(1)} collective-permute-done((bf16[2,128,768]{2,1,0:T(8,128)(2,1)}, bf16[2,128,768]{2,1,0:T(8,128)(2,1)S(1)}, u32[]{:S(2)}, u32[]{:S(2)}) %collective-permute-start.17) | collective-permute-done | bytes 393248 | tf_op jit(solution)/shard_map/ppermute | solution.py:91
  138.0 2.0 pad_maximum_fusion.3
  140.0 2.7 %gather_fusion.2 = bf16[4,128,768]{2,1,0:T(8,128)(2,1)} fusion(bf16[4,128,768]{2,1,0:T(8,128)(2,1)} %pad_maximum_fusion.3, s32[1024]{0:T(1024)S(1)} %pad_clamp_fusion.1), kind=kCustom, calls=%fused_computation.2 | custom fusion | bytes 1572880 | tf_op jit(solution)/shard_map/gather | solution.py:92
  143.7 1.4 collective-permute-start.22
  145.7 2.3 %copy-done.2 = bf16[384,6144]{1,0:T(8,128)(2,1)S(1)} copy-done((bf16[384,6144]{1,0:T(8,128)(2,1)S(1)}, bf16[384,6144]{1,0:T(8,128)(2,1)}, u32[]{:S(2)}) %copy-start.2) | copy-done | bytes 4718616
  148.1 6.6 %shard_map.86 = (bf16[256,384]{1,0:T(8,128)(2,1)S(1)}, bf16[256,384]{1,0:T(8,128)(2,1)}) custom-call(bf16[32,6144]{1,0:T(8,128)(2,1)S(1)} %collective-permute-done.18.refs_0_, bf16[32,6144]{1,0:T(8,128)(2,1)S(1)} %collective-permute-done.19.refs_1_, bf16[32,6144]{1,0:T(8,128)(2,1)S(1)} %collective-permute-done.20.refs_2_, ...), custom_call_target="tpu_custom_call" | custom-call | flops 2415919104 | bytes 12582912 | tf_op jit(solution)/shard_map/pallas_call | solution.py:133
  155.4 7.7 %collective-permute-done.21 = bf16[512,384]{1,0:T(8,128)(2,1)} collective-permute-done((bf16[512,384]{1,0:T(8,128)(2,1)}, bf16[512,384]{1,0:T(8,128)(2,1)}, u32[]{:S(2)}, u32[]{:S(2)}) %collective-permute-start.21) | collective-permute-done | bytes 393248 | tf_op jit(solution)/shard_map/ppermute | solution.py:36
  163.1 3.0 %collective-permute-done.24 = bf16[512,384]{1,0:T(8,128)(2,1)S(1)} collective-permute-done((bf16[512,384]{1,0:T(8,128)(2,1)}, bf16[512,384]{1,0:T(8,128)(2,1)S(1)}, u32[]{:S(2)}, u32[]{:S(2)}) %collective-permute-start.24) | collective-permute-done | bytes 393248 | tf_op jit(solution)/shard_map/ppermute | solution.py:40
  169.9 3.8 %fusion.14 = f32[768,384]{1,0:T(8,128)S(1)} fusion(bf16[2048,768]{1,0:T(8,128)(2,1)} %all-gather.3.cloned.1.call-done, bf16[2048,384]{1,0:T(8,128)(2,1)S(1)} %bitcast.75), kind=kOutput, calls=%fused_computation.48 | convolution fusion | flops 1207959552 | bytes 5898240 | tf_op jit(solution)/shard_map/dot_general | solution.py:100
  177.2 10.1 %collective-permute-done.27 = bf16[512,384]{1,0:T(8,128)(2,1)} collective-permute-done((bf16[512,384]{1,0:T(8,128)(2,1)}, bf16[512,384]{1,0:T(8,128)(2,1)}, u32[]{:S(2)}, u32[]{:S(2)}) %collective-permute-start.27) | collective-permute-done | bytes 393248 | tf_op jit(solution)/shard_map/ppermute | solution.py:40
  187.4 1.4 pad_maximum_fusion.1
  188.8 3.7 %fusion.15 = f32[768,384]{1,0:T(8,128)S(1)} fusion(bf16[2048,768]{1,0:T(8,128)(2,1)} %all-gather.5.cloned.1.call-done, bf16[2048,384]{1,0:T(8,128)(2,1)S(1)} %bitcast.76), kind=kOutput, calls=%fused_computation.49 | convolution fusion | flops 1207959552 | bytes 5898240 | tf_op jit(solution)/shard_map/dot_general | solution.py:100
  193.3 1.6 collective-permute-done.29
  (95 shorter events, 27.2 us)
Async XLA Ops:
  7.2 162.7 %all-gather.3.cloned.1.call-start = ((), (), s32[]{:S(2)}) async-start(), calls=%async_computation.1 | async-start | bytes 3932160 | tf_op jit(solution)/shard_map/all_gather | solution.py:96
  8.9 8.4 %collective-permute-start = (bf16[2,128,384]{2,1,0:T(8,128)(2,1)S(1)}, bf16[2,128,384]{2,1,0:T(8,128)(2,1)S(1)}, u32[]{:S(2)}, u32[]{:S(2)}) collective-permute-start(bf16[2,128,384]{2,1,0:T(8,128)(2,1)S(1)} %get-tuple-element.114), channel_id=1, source_target_pairs={{0,1},{1,0},{2,3},{3,2},{4,5},{5,4},{6,7},{7,6},{8,9},{9,8},{10,11... | collective-permute-start | bytes 589832 | tf_op jit(solution)/shard_map/ppermute | solution.py:32
  17.2 3.5 %collective-permute-start.1 = (bf16[128,6144]{1,0:T(8,128)(2,1)S(1)}, bf16[128,6144]{1,0:T(8,128)(2,1)S(1)}, u32[]{:S(2)}, u32[]{:S(2)}) collective-permute-start(bf16[128,6144]{1,0:T(8,128)(2,1)S(1)} %get-tuple-element.52), channel_id=1, source_target_pairs={{0,1},{1,0},{2,3},{3,2},{4,5},{5,4},{6,7},{7,6},{8,9},{9,8},{10,11... | collective-permute-start | bytes 4718600 | tf_op jit(solution)/shard_map/ppermute | solution.py:32
  17.4 10.7 %collective-permute-start.7 = (bf16[2,128,768]{2,1,0:T(8,128)(2,1)S(1)}, bf16[2,128,768]{2,1,0:T(8,128)(2,1)S(1)}, u32[]{:S(2)}, u32[]{:S(2)}) collective-permute-start(bf16[2,128,768]{2,1,0:T(8,128)(2,1)S(1)} %get-tuple-element.111), channel_id=1, source_target_pairs={{0,64},{16,80},{32,96},{48,112},{64,0},{80,16},{96,32},{112,48},{1... | collective-permute-start | bytes 1179656 | tf_op jit(solution)/shard_map/ppermute | solution.py:167
  21.2 20.3 %collective-permute-start.2 = (bf16[32,6144]{1,0:T(8,128)(2,1)S(1)}, bf16[32,6144]{1,0:T(8,128)(2,1)S(1)}, u32[]{:S(2)}, u32[]{:S(2)}) collective-permute-start(bf16[32,6144]{1,0:T(8,128)(2,1)S(1)} %get-tuple-element.104), channel_id=1, source_target_pairs={{0,2},{1,3},{2,4},{3,5},{4,6},{5,7},{6,0},{7,1},{8,10},{9,11},{10,... | collective-permute-start | bytes 1179656 | tf_op jit(solution)/shard_map/ppermute | solution.py:40
  21.3 20.2 %collective-permute-start.3 = (bf16[32,6144]{1,0:T(8,128)(2,1)S(1)}, bf16[32,6144]{1,0:T(8,128)(2,1)S(1)}, u32[]{:S(2)}, u32[]{:S(2)}) collective-permute-start(bf16[32,6144]{1,0:T(8,128)(2,1)S(1)} %get-tuple-element.106), channel_id=1, source_target_pairs={{0,4},{1,5},{2,6},{3,7},{4,0},{5,1},{6,2},{7,3},{8,12},{9,13},{10,... | collective-permute-start | bytes 1179656 | tf_op jit(solution)/shard_map/ppermute | solution.py:40
  23.2 18.6 %collective-permute-start.4 = (bf16[32,6144]{1,0:T(8,128)(2,1)S(1)}, bf16[32,6144]{1,0:T(8,128)(2,1)S(1)}, u32[]{:S(2)}, u32[]{:S(2)}) collective-permute-start(bf16[32,6144]{1,0:T(8,128)(2,1)S(1)} %get-tuple-element.105), channel_id=1, source_target_pairs={{0,6},{1,7},{2,0},{3,1},{4,2},{5,3},{6,4},{7,5},{8,14},{9,15},{10,... | collective-permute-start | bytes 1179656 | tf_op jit(solution)/shard_map/ppermute | solution.py:40
  27.0 15.7 %collective-permute-start.5 = (bf16[128,6144]{1,0:T(8,128)(2,1)S(1)}, bf16[128,6144]{1,0:T(8,128)(2,1)S(1)}, u32[]{:S(2)}, u32[]{:S(2)}) collective-permute-start(bf16[128,6144]{1,0:T(8,128)(2,1)S(1)} %get-tuple-element.56), channel_id=1, source_target_pairs={{0,1},{1,0},{2,3},{3,2},{4,5},{5,4},{6,7},{7,6},{8,9},{9,8},{10,11... | collective-permute-start | bytes 4718600 | tf_op jit(solution)/shard_map/ppermute | solution.py:32
  28.9 23.8 %collective-permute-start.8 = (bf16[2,128,768]{2,1,0:T(8,128)(2,1)S(1)}, bf16[2,128,768]{2,1,0:T(8,128)(2,1)S(1)}, u32[]{:S(2)}, u32[]{:S(2)}) collective-permute-start(bf16[2,128,768]{2,1,0:T(8,128)(2,1)S(1)} %get-tuple-element.110), channel_id=1, source_target_pairs={{0,128},{16,144},{32,160},{48,176},{64,192},{80,208},{96,224},{112... | collective-permute-start | bytes 1179656 | tf_op jit(solution)/shard_map/ppermute | solution.py:91
  43.2 11.1 %collective-permute-start.10 = (bf16[32,6144]{1,0:T(8,128)(2,1)S(1)}, bf16[32,6144]{1,0:T(8,128)(2,1)}, u32[]{:S(2)}, u32[]{:S(2)}) collective-permute-start(bf16[32,6144]{1,0:T(8,128)(2,1)S(1)} %get-tuple-element.101), channel_id=1, source_target_pairs={{0,4},{1,5},{2,6},{3,7},{4,0},{5,1},{6,2},{7,3},{8,12},{9,13},{10,... | collective-permute-start | bytes 1179656 | tf_op jit(solution)/shard_map/ppermute | solution.py:40
  44.3 20.0 %collective-permute-start.11 = (bf16[32,6144]{1,0:T(8,128)(2,1)S(1)}, bf16[32,6144]{1,0:T(8,128)(2,1)}, u32[]{:S(2)}, u32[]{:S(2)}) collective-permute-start(bf16[32,6144]{1,0:T(8,128)(2,1)S(1)} %get-tuple-element.100), channel_id=1, source_target_pairs={{0,6},{1,7},{2,0},{3,1},{4,2},{5,3},{6,4},{7,5},{8,14},{9,15},{10,... | collective-permute-start | bytes 1179656 | tf_op jit(solution)/shard_map/ppermute | solution.py:40
  46.8 17.5 %collective-permute-start.9 = (bf16[32,6144]{1,0:T(8,128)(2,1)S(1)}, bf16[32,6144]{1,0:T(8,128)(2,1)}, u32[]{:S(2)}, u32[]{:S(2)}) collective-permute-start(bf16[32,6144]{1,0:T(8,128)(2,1)S(1)} %get-tuple-element.102), channel_id=1, source_target_pairs={{0,2},{1,3},{2,4},{3,5},{4,6},{5,7},{6,0},{7,1},{8,10},{9,11},{10,... | collective-permute-start | bytes 1179656 | tf_op jit(solution)/shard_map/ppermute | solution.py:40
  47.0 17.4 %collective-permute-start.6 = (bf16[32,6144]{1,0:T(8,128)(2,1)}, bf16[32,6144]{1,0:T(8,128)(2,1)}, u32[]{:S(2)}, u32[]{:S(2)}) collective-permute-start(bf16[32,6144]{1,0:T(8,128)(2,1)} %add_convert_fusion.2), channel_id=1, source_target_pairs={{0,8},{1,9},{2,10},{3,11},{4,12},{5,13},{6,14},{7,15},{8,0},{9,1},... | collective-permute-start | bytes 1179656 | tf_op jit(solution)/shard_map/ppermute | solution.py:36
  68.1 35.4 %collective-permute-start.13 = (bf16[384,6144]{1,0:T(8,128)(2,1)}, bf16[384,6144]{1,0:T(8,128)(2,1)}, u32[]{:S(2)}, u32[]{:S(2)}) collective-permute-start(bf16[384,6144]{1,0:T(8,128)(2,1)} %refs_8_.1), channel_id=1, source_target_pairs={{0,1},{1,0},{2,3},{3,2},{4,5},{5,4},{6,7},{7,6},{8,9},{9,8},{10,11... | collective-permute-start | bytes 14155784 | tf_op jit(solution)/shard_map/ppermute | solution.py:32
  69.4 14.7 %collective-permute-start.12 = (bf16[32,6144]{1,0:T(8,128)(2,1)S(1)}, bf16[32,6144]{1,0:T(8,128)(2,1)S(1)}, u32[]{:S(2)}, u32[]{:S(2)}) collective-permute-start(bf16[32,6144]{1,0:T(8,128)(2,1)S(1)} %get-tuple-element.67.refs_7_), channel_id=1, source_target_pairs={{0,8},{1,9},{2,10},{3,11},{4,12},{5,13},{6,14},{7,15},{8,0},{9,1},... | collective-permute-start | bytes 1179656 | tf_op jit(solution)/shard_map/ppermute | solution.py:36
  74.6 24.3 %collective-permute-start.14 = (bf16[32,6144]{1,0:T(8,128)(2,1)S(1)}, bf16[32,6144]{1,0:T(8,128)(2,1)S(1)}, u32[]{:S(2)}, u32[]{:S(2)}) collective-permute-start(bf16[32,6144]{1,0:T(8,128)(2,1)S(1)} %get-tuple-element.67.refs_7_), channel_id=1, source_target_pairs={{0,6},{1,7},{2,0},{3,1},{4,2},{5,3},{6,4},{7,5},{8,14},{9,15},{10,... | collective-permute-start | bytes 1179656 | tf_op jit(solution)/shard_map/ppermute | solution.py:40
  82.4 16.5 %collective-permute-start.15 = (bf16[32,6144]{1,0:T(8,128)(2,1)S(1)}, bf16[32,6144]{1,0:T(8,128)(2,1)S(1)}, u32[]{:S(2)}, u32[]{:S(2)}) collective-permute-start(bf16[32,6144]{1,0:T(8,128)(2,1)S(1)} %get-tuple-element.67.refs_7_), channel_id=1, source_target_pairs={{0,4},{1,5},{2,6},{3,7},{4,0},{5,1},{6,2},{7,3},{8,12},{9,13},{10,... | collective-permute-start | bytes 1179656 | tf_op jit(solution)/shard_map/ppermute | solution.py:40
  83.1 20.3 %collective-permute-start.16 = (bf16[32,6144]{1,0:T(8,128)(2,1)S(1)}, bf16[32,6144]{1,0:T(8,128)(2,1)S(1)}, u32[]{:S(2)}, u32[]{:S(2)}) collective-permute-start(bf16[32,6144]{1,0:T(8,128)(2,1)S(1)} %get-tuple-element.67.refs_7_), channel_id=1, source_target_pairs={{0,2},{1,3},{2,4},{3,5},{4,6},{5,7},{6,0},{7,1},{8,10},{9,11},{10,... | collective-permute-start | bytes 1179656 | tf_op jit(solution)/shard_map/ppermute | solution.py:40
  104.6 38.1 %all-to-all-start = ((bf16[16,32,384]{2,1,0:T(8,128)(2,1)}), bf16[16,32,384]{2,1,0:T(8,128)(2,1)}, u32[]{:S(2)}, u32[]{:S(2)}) async-start(bf16[16,32,384]{2,1,0:T(8,128)(2,1)} %bitcast.29), calls=%async_computation | async-start | bytes 786432 | tf_op jit(solution)/shard_map/all_to_all | solution.py:200
  110.1 78.7 %all-gather.5.cloned.1.call-start = ((), (), s32[]{:S(2)}) async-start(), calls=%async_computation.2 | async-start | bytes 3932160 | tf_op jit(solution)/shard_map/all_gather | solution.py:96
  110.2 27.9 %collective-permute-start.17 = (bf16[2,128,768]{2,1,0:T(8,128)(2,1)}, bf16[2,128,768]{2,1,0:T(8,128)(2,1)S(1)}, u32[]{:S(2)}, u32[]{:S(2)}) collective-permute-start(bf16[2,128,768]{2,1,0:T(8,128)(2,1)} %get-tuple-element.68), channel_id=1, source_target_pairs={{0,128},{16,144},{32,160},{48,176},{64,192},{80,208},{96,224},{112... | collective-permute-start | bytes 1179656 | tf_op jit(solution)/shard_map/ppermute | solution.py:91
  112.5 30.2 %collective-permute-start.18 = (bf16[32,6144]{1,0:T(8,128)(2,1)S(1)}, bf16[32,6144]{1,0:T(8,128)(2,1)S(1)}, u32[]{:S(2)}, u32[]{:S(2)}) collective-permute-start(bf16[32,6144]{1,0:T(8,128)(2,1)S(1)} %collective-permute-done.12.refs_3_), channel_id=1, source_target_pairs={{0,6},{1,7},{2,0},{3,1},{4,2},{5,3},{6,4},{7,5},{8,14},{9,15},{10,... | collective-permute-start | bytes 1179656 | tf_op jit(solution)/shard_map/ppermute | solution.py:40
  112.5 30.2 %collective-permute-start.19 = (bf16[32,6144]{1,0:T(8,128)(2,1)S(1)}, bf16[32,6144]{1,0:T(8,128)(2,1)S(1)}, u32[]{:S(2)}, u32[]{:S(2)}) collective-permute-start(bf16[32,6144]{1,0:T(8,128)(2,1)S(1)} %collective-permute-done.12.refs_3_), channel_id=1, source_target_pairs={{0,4},{1,5},{2,6},{3,7},{4,0},{5,1},{6,2},{7,3},{8,12},{9,13},{10,... | collective-permute-start | bytes 1179656 | tf_op jit(solution)/shard_map/ppermute | solution.py:40
  112.9 29.7 %collective-permute-start.20 = (bf16[32,6144]{1,0:T(8,128)(2,1)S(1)}, bf16[32,6144]{1,0:T(8,128)(2,1)S(1)}, u32[]{:S(2)}, u32[]{:S(2)}) collective-permute-start(bf16[32,6144]{1,0:T(8,128)(2,1)S(1)} %collective-permute-done.12.refs_3_), channel_id=1, source_target_pairs={{0,2},{1,3},{2,4},{3,5},{4,6},{5,7},{6,0},{7,1},{8,10},{9,11},{10,... | collective-permute-start | bytes 1179656 | tf_op jit(solution)/shard_map/ppermute | solution.py:40
  142.9 20.2 %collective-permute-start.21 = (bf16[512,384]{1,0:T(8,128)(2,1)}, bf16[512,384]{1,0:T(8,128)(2,1)}, u32[]{:S(2)}, u32[]{:S(2)}) collective-permute-start(bf16[512,384]{1,0:T(8,128)(2,1)} %bitcast.30), channel_id=1, source_target_pairs={{0,8},{1,9},{2,10},{3,11},{4,12},{5,13},{6,14},{7,15},{8,0},{9,1},... | collective-permute-start | bytes 1179656 | tf_op jit(solution)/shard_map/ppermute | solution.py:36
  143.7 19.4 %collective-permute-start.22 = (bf16[512,384]{1,0:T(8,128)(2,1)}, bf16[512,384]{1,0:T(8,128)(2,1)S(1)}, u32[]{:S(2)}, u32[]{:S(2)}) collective-permute-start(bf16[512,384]{1,0:T(8,128)(2,1)} %bitcast.30), channel_id=1, source_target_pairs={{0,6},{1,7},{2,0},{3,1},{4,2},{5,3},{6,4},{7,5},{8,14},{9,15},{10,... | collective-permute-start | bytes 1179656 | tf_op jit(solution)/shard_map/ppermute | solution.py:40
  145.1 18.0 %collective-permute-start.23 = (bf16[512,384]{1,0:T(8,128)(2,1)}, bf16[512,384]{1,0:T(8,128)(2,1)S(1)}, u32[]{:S(2)}, u32[]{:S(2)}) collective-permute-start(bf16[512,384]{1,0:T(8,128)(2,1)} %bitcast.30), channel_id=1, source_target_pairs={{0,4},{1,5},{2,6},{3,7},{4,0},{5,1},{6,2},{7,3},{8,12},{9,13},{10,... | collective-permute-start | bytes 1179656 | tf_op jit(solution)/shard_map/ppermute | solution.py:40
  145.2 20.8 %collective-permute-start.24 = (bf16[512,384]{1,0:T(8,128)(2,1)}, bf16[512,384]{1,0:T(8,128)(2,1)S(1)}, u32[]{:S(2)}, u32[]{:S(2)}) collective-permute-start(bf16[512,384]{1,0:T(8,128)(2,1)} %bitcast.30), channel_id=1, source_target_pairs={{0,2},{1,3},{2,4},{3,5},{4,6},{5,7},{6,0},{7,1},{8,10},{9,11},{10,... | collective-permute-start | bytes 1179656 | tf_op jit(solution)/shard_map/ppermute | solution.py:40
  166.1 10.4 %collective-permute-start.25 = (bf16[512,384]{1,0:T(8,128)(2,1)}, bf16[512,384]{1,0:T(8,128)(2,1)S(1)}, u32[]{:S(2)}, u32[]{:S(2)}) collective-permute-start(bf16[512,384]{1,0:T(8,128)(2,1)} %collective-permute-done.21), channel_id=1, source_target_pairs={{0,6},{1,7},{2,0},{3,1},{4,2},{5,3},{6,4},{7,5},{8,14},{9,15},{10,... | collective-permute-start | bytes 1179656 | tf_op jit(solution)/shard_map/ppermute | solution.py:40
  166.1 11.1 %collective-permute-start.26 = (bf16[512,384]{1,0:T(8,128)(2,1)}, bf16[512,384]{1,0:T(8,128)(2,1)}, u32[]{:S(2)}, u32[]{:S(2)}) collective-permute-start(bf16[512,384]{1,0:T(8,128)(2,1)} %collective-permute-done.21), channel_id=1, source_target_pairs={{0,4},{1,5},{2,6},{3,7},{4,0},{5,1},{6,2},{7,3},{8,12},{9,13},{10,... | collective-permute-start | bytes 1179656 | tf_op jit(solution)/shard_map/ppermute | solution.py:40
  166.5 20.8 %collective-permute-start.27 = (bf16[512,384]{1,0:T(8,128)(2,1)}, bf16[512,384]{1,0:T(8,128)(2,1)}, u32[]{:S(2)}, u32[]{:S(2)}) collective-permute-start(bf16[512,384]{1,0:T(8,128)(2,1)} %collective-permute-done.21), channel_id=1, source_target_pairs={{0,2},{1,3},{2,4},{3,5},{4,6},{5,7},{6,0},{7,1},{8,10},{9,11},{10,... | collective-permute-start | bytes 1179656 | tf_op jit(solution)/shard_map/ppermute | solution.py:40
  167.5 6.2 %collective-permute-start.28 = (bf16[256,384]{1,0:T(8,128)(2,1)}, bf16[256,384]{1,0:T(8,128)(2,1)}, u32[]{:S(2)}, u32[]{:S(2)}) collective-permute-start(bf16[256,384]{1,0:T(8,128)(2,1)} %get-tuple-element.87), channel_id=1, source_target_pairs={{0,1},{1,0},{2,3},{3,2},{4,5},{5,4},{6,7},{7,6},{8,9},{9,8},{10,11... | collective-permute-start | bytes 589832 | tf_op jit(solution)/shard_map/ppermute | solution.py:32
  (9 other events, 94.5 us)
Sparse Core Ops, SparseCore 0:
  69.5 51.4 all-gather.2
  142.8 38.1 all-gather.4

commit v3 on v2

--- a/solution.py
+++ b/solution.py
@@ -87,9 +87,9 @@
     return [to_x(b, 3), to_x(b, 2), to_x(b, 1), b]
 
 
-def spread_z(v, order):
+def spread_z(v):
     four = jnp.concatenate([v, lax.ppermute(v, "dp", dp_swap(2))])
-    return four[order].reshape(-1, v.shape[-1])
+    return four.reshape(-1, v.shape[-1])
 
 
 def gather_y(v):
@@ -166,7 +166,7 @@
     pair = jnp.concatenate([ctx[1::2], there], axis=-1)
     two = jnp.stack([pair, lax.ppermute(pair, "dp", dp_swap(1))])
     order_z = (lax.axis_index("dp") // 4) ^ jnp.arange(4)
-    near_z = spread_z(two[:, 1], order_z)
+    near_z = spread_z(two[:, 1])
     ctx_low, from0 = after(ctx[2:], from0)
     sent0 = send_x(add(own0, from0).astype(BF16))
     other1, own1 = project(ctx_low.reshape(2 * quarter, width), w_out)
@@ -198,7 +198,8 @@
     far0, far_z, w_sibling, *near = after(far0, far_z, w_sibling, *near)
     blocks = near[3].reshape(r, 4, 4, width).transpose(2, 1, 0, 3).reshape(rows, width)
     turned = lax.all_to_all(blocks, "dp", 0, 0, axis_index_groups=Y_THEN_Z, tiled=True)
-    far_z = spread_z(far_z, order_z)
+    turned = turned.reshape(4, 4, r, width)[:, order_z].reshape(rows, width)
+    far_z = spread_z(far_z)
     far = gather_x(far0)
     turned, far_z, *far = after(turned, far_z, *far)
     ctx_far = gather_y(far_z)

time: 203 us -> 202 us (level)
  other arithmetic: 13 us -> 10.7 us
    unnamed x16 -> x20, local copies, waits for them, and re-layouts: 6.05 us -> 6.33 us
  transfers between devices with their start and end apart: 33 -> 33, of which waited for: 15 -> 16; matrix products, arithmetic and copies ran while one was open for 9% -> 9% of each run, Pallas kernels for 6% -> 6%
where the time goes in v3:
time: 202 us
  waiting for transfers between devices  91.8 us (45%)
  starting transfers between devices  51.3 us (25%)
  between operations  14.6 us (7%)
  local copies, waits for them, and re-layouts  14.1 us (7%)
  Pallas kernels  11.9 us (6%)
  other arithmetic  10.7 us (5%)
  matrix products  7.47 us (4%)
    ppermute x18, waiting for transfers between devices, to_x(): return lax.ppermute(a, 'mp', mp_perm(dx=dx))  53.6 us
    ppermute x2, waiting for transfers between devices, spread_z(): four = jnp.concatenate([v, lax.ppermute(v, 'dp', dp_swap(2))])  24.1 us
    ppermute x18, starting transfers between devices, to_x(): return lax.ppermute(a, 'mp', mp_perm(dx=dx))  20.4 us
    ppermute x3, starting transfers between devices, to_z(): return lax.ppermute(a, 'mp', mp_perm(dz=1))  11.6 us
    ppermute x3, waiting for transfers between devices, to_z(): return lax.ppermute(a, 'mp', mp_perm(dz=1))  9.11 us
    ppermute x6, starting transfers between devices, to_core(): return lax.ppermute(a, 'mp', mp_perm(dc=1))  7.6 us
    dot_general x2, matrix products, contract_rows(): lax.dot_general(a, b, (((0,), (0,)), ((), ())), preferred_element_type=F32)  7.47 us
    pallas_call x1, Pallas kernels, back_project(): pl.pallas_call(back_project_kernel, grid=(features // tile,), in_specs=[b...  6.58 us
  transfers between devices with their start and end apart: 33, of which 16 were waited for; matrix products, arithmetic and copies ran while one was open for 9% of the time, Pallas kernels for 6%

profile of v3, /device:TPU:1, one launch (start us, length us, event | category | flops | bytes accessed | tf_op | source)
XLA Modules:
  0.0 201.8 jit_solution(16722154043727516837)
XLA Ops:
  8.9 3.3 %collective-permute-start = (bf16[2,128,384]{2,1,0:T(8,128)(2,1)S(1)}, bf16[2,128,384]{2,1,0:T(8,128)(2,1)S(1)}, u32[]{:S(2)}, u32[]{:S(2)}) collective-permute-start(bf16[2,128,384]{2,1,0:T(8,128)(2,1)S(1)} %get-tuple-element.114), channel_id=1, source_target_pairs={{0,1},{1,0},{2,3},{3,2},{4,5},{5,4},{6,7},{7,6},{8,9},{9,8},{10,11... | collective-permute-start | bytes 589832 | tf_op jit(solution)/shard_map/ppermute | solution.py:32
  12.2 2.3 %copy-done.1 = bf16[384,6144]{1,0:T(8,128)(2,1)S(1)} copy-done((bf16[384,6144]{1,0:T(8,128)(2,1)S(1)}, bf16[384,6144]{1,0:T(8,128)(2,1)}, u32[]{:S(2)}) %copy-start.1) | copy-done | bytes 4718616
  14.6 2.7 %shard_map.84 = (bf16[128,6144]{1,0:T(8,128)(2,1)S(1)}, bf16[128,6144]{1,0:T(8,128)(2,1)S(1)}) custom-call(bf16[256,384]{1,0:T(8,128)(2,1)S(1)} %bitcast.76, bf16[384,6144]{1,0:T(8,128)(2,1)S(1)} %copy-done.1), custom_call_target="tpu_custom_call" | custom-call | flops 1207959552 | bytes 7864320 | tf_op jit(solution)/shard_map/pallas_call | solution.py:63
  17.5 3.2 %collective-permute-done.1 = bf16[128,6144]{1,0:T(8,128)(2,1)S(1)} collective-permute-done((bf16[128,6144]{1,0:T(8,128)(2,1)S(1)}, bf16[128,6144]{1,0:T(8,128)(2,1)S(1)}, u32[]{:S(2)}, u32[]{:S(2)}) %collective-permute-start.1) | collective-permute-done | bytes 1572896 | tf_op jit(solution)/shard_map/ppermute | solution.py:32
  21.3 1.9 collective-permute-start.3
  24.4 2.7 %shard_map.85 = (bf16[128,6144]{1,0:T(8,128)(2,1)S(1)}, bf16[128,6144]{1,0:T(8,128)(2,1)S(1)}) custom-call(bf16[256,384]{1,0:T(8,128)(2,1)S(1)} %bitcast.75, bf16[384,6144]{1,0:T(8,128)(2,1)S(1)} %copy-done.1), custom_call_target="tpu_custom_call" | custom-call | flops 1207959552 | bytes 7864320 | tf_op jit(solution)/shard_map/pallas_call | solution.py:63
  28.9 3.0 %collective-permute-start.8 = (bf16[2,128,768]{2,1,0:T(8,128)(2,1)S(1)}, bf16[2,128,768]{2,1,0:T(8,128)(2,1)S(1)}, u32[]{:S(2)}, u32[]{:S(2)}) collective-permute-start(bf16[2,128,768]{2,1,0:T(8,128)(2,1)S(1)} %get-tuple-element.110), channel_id=1, source_target_pairs={{0,128},{16,144},{32,160},{48,176},{64,192},{80,208},{96,224},{112... | collective-permute-start | bytes 1179656 | tf_op jit(solution)/shard_map/ppermute | solution.py:91
  31.9 9.6 %collective-permute-done.2 = bf16[32,6144]{1,0:T(8,128)(2,1)S(1)} collective-permute-done((bf16[32,6144]{1,0:T(8,128)(2,1)S(1)}, bf16[32,6144]{1,0:T(8,128)(2,1)S(1)}, u32[]{:S(2)}, u32[]{:S(2)}) %collective-permute-start.2) | collective-permute-done | bytes 393248 | tf_op jit(solution)/shard_map/ppermute | solution.py:40
  43.6 2.5 %collective-permute-start.11 = (bf16[32,6144]{1,0:T(8,128)(2,1)S(1)}, bf16[32,6144]{1,0:T(8,128)(2,1)S(1)}, u32[]{:S(2)}, u32[]{:S(2)}) collective-permute-start(bf16[32,6144]{1,0:T(8,128)(2,1)S(1)} %get-tuple-element.100), channel_id=1, source_target_pairs={{0,6},{1,7},{2,0},{3,1},{4,2},{5,3},{6,4},{7,5},{8,14},{9,15},{10,... | collective-permute-start | bytes 1179656 | tf_op jit(solution)/shard_map/ppermute | solution.py:40
  46.3 5.7 %collective-permute-start.6 = (bf16[32,6144]{1,0:T(8,128)(2,1)S(1)}, bf16[32,6144]{1,0:T(8,128)(2,1)S(1)}, u32[]{:S(2)}, u32[]{:S(2)}) collective-permute-start(bf16[32,6144]{1,0:T(8,128)(2,1)S(1)} %add_convert_fusion.2), channel_id=1, source_target_pairs={{0,8},{1,9},{2,10},{3,11},{4,12},{5,13},{6,14},{7,15},{8,0},{9,1},... | collective-permute-start | bytes 1179656 | tf_op jit(solution)/shard_map/ppermute | solution.py:36
  53.5 10.0 %collective-permute-done.11 = bf16[32,6144]{1,0:T(8,128)(2,1)S(1)} collective-permute-done((bf16[32,6144]{1,0:T(8,128)(2,1)S(1)}, bf16[32,6144]{1,0:T(8,128)(2,1)S(1)}, u32[]{:S(2)}, u32[]{:S(2)}) %collective-permute-start.11) | collective-permute-done | bytes 393248 | tf_op jit(solution)/shard_map/ppermute | solution.py:40
  67.3 5.3 %collective-permute-start.12 = (bf16[32,6144]{1,0:T(8,128)(2,1)S(1)}, bf16[32,6144]{1,0:T(8,128)(2,1)S(1)}, u32[]{:S(2)}, u32[]{:S(2)}) collective-permute-start(bf16[32,6144]{1,0:T(8,128)(2,1)S(1)} %get-tuple-element.67.refs_7_), channel_id=1, source_target_pairs={{0,8},{1,9},{2,10},{3,11},{4,12},{5,13},{6,14},{7,15},{8,0},{9,1},... | collective-permute-start | bytes 1179656 | tf_op jit(solution)/shard_map/ppermute | solution.py:36
  72.6 7.6 %collective-permute-start.14 = (bf16[32,6144]{1,0:T(8,128)(2,1)S(1)}, bf16[32,6144]{1,0:T(8,128)(2,1)S(1)}, u32[]{:S(2)}, u32[]{:S(2)}) collective-permute-start(bf16[32,6144]{1,0:T(8,128)(2,1)S(1)} %get-tuple-element.67.refs_7_), channel_id=1, source_target_pairs={{0,6},{1,7},{2,0},{3,1},{4,2},{5,3},{6,4},{7,5},{8,14},{9,15},{10,... | collective-permute-start | bytes 1179656 | tf_op jit(solution)/shard_map/ppermute | solution.py:40
  80.7 1.9 collective-permute-done.12.refs_3_
  82.6 14.2 %collective-permute-done.14.refs_4_ = bf16[32,6144]{1,0:T(8,128)(2,1)S(1)} collective-permute-done((bf16[32,6144]{1,0:T(8,128)(2,1)S(1)}, bf16[32,6144]{1,0:T(8,128)(2,1)S(1)}, u32[]{:S(2)}, u32[]{:S(2)}) %collective-permute-start.14) | collective-permute-done | bytes 393248 | tf_op jit(solution)/shard_map/ppermute | solution.py:40
  96.8 3.8 %collective-permute-done.16.refs_6_ = bf16[32,6144]{1,0:T(8,128)(2,1)S(1)} collective-permute-done((bf16[32,6144]{1,0:T(8,128)(2,1)S(1)}, bf16[32,6144]{1,0:T(8,128)(2,1)S(1)}, u32[]{:S(2)}, u32[]{:S(2)}) %collective-permute-start.16) | collective-permute-done | bytes 393248 | tf_op jit(solution)/shard_map/ppermute | solution.py:40
  101.7 6.2 %all-to-all-start = ((bf16[16,32,384]{2,1,0:T(8,128)(2,1)}), bf16[16,32,384]{2,1,0:T(8,128)(2,1)}, u32[]{:S(2)}, u32[]{:S(2)}) async-start(bf16[16,32,384]{2,1,0:T(8,128)(2,1)} %bitcast.28), calls=%async_computation | async-start | bytes 786432 | tf_op jit(solution)/shard_map/all_to_all | solution.py:200
  108.0 2.3 %collective-permute-start.17 = (bf16[2,128,768]{2,1,0:T(8,128)(2,1)}, bf16[2,128,768]{2,1,0:T(8,128)(2,1)}, u32[]{:S(2)}, u32[]{:S(2)}) collective-permute-start(bf16[2,128,768]{2,1,0:T(8,128)(2,1)} %get-tuple-element.68), channel_id=1, source_target_pairs={{0,128},{16,144},{32,160},{48,176},{64,192},{80,208},{96,224},{112... | collective-permute-start | bytes 1179656 | tf_op jit(solution)/shard_map/ppermute | solution.py:91
  111.9 24.1 %collective-permute-done.17 = bf16[2,128,768]{2,1,0:T(8,128)(2,1)} collective-permute-done((bf16[2,128,768]{2,1,0:T(8,128)(2,1)}, bf16[2,128,768]{2,1,0:T(8,128)(2,1)}, u32[]{:S(2)}, u32[]{:S(2)}) %collective-permute-start.17) | collective-permute-done | bytes 393248 | tf_op jit(solution)/shard_map/ppermute | solution.py:91
  136.0 2.1 %pad_maximum_fusion.3 = bf16[4,128,768]{2,1,0:T(8,128)(2,1)} fusion(bf16[2,128,768]{2,1,0:T(8,128)(2,1)} %collective-permute-done.17, bf16[2,128,768]{2,1,0:T(8,128)(2,1)} %get-tuple-element.68), kind=kLoop, calls=%fused_computation.10 | loop fusion | flops 393216 | bytes 1572864 | tf_op jit(solution)/shard_map/concatenate | solution.py:91
  138.1 2.3 %gather_fusion.1 = bf16[4,4,32,384]{3,2,1,0:T(8,128)(2,1)} fusion(bf16[4,4,32,384]{3,2,1,0:T(8,128)(2,1)} %bitcast.29, s32[1024]{0:T(1024)S(1)} %pad_clamp_fusion.1), kind=kCustom, calls=%fused_computation.1 | custom fusion | bytes 786448 | tf_op jit(solution)/shard_map/gather | solution.py:201
  140.4 1.8 copy.11
  143.1 1.4 collective-permute-start.22
  145.4 2.3 %copy-done.2 = bf16[384,6144]{1,0:T(8,128)(2,1)S(1)} copy-done((bf16[384,6144]{1,0:T(8,128)(2,1)S(1)}, bf16[384,6144]{1,0:T(8,128)(2,1)}, u32[]{:S(2)}) %copy-start.2) | copy-done | bytes 4718616
  147.7 6.6 %shard_map.86 = (bf16[256,384]{1,0:T(8,128)(2,1)S(1)}, bf16[256,384]{1,0:T(8,128)(2,1)}) custom-call(bf16[32,6144]{1,0:T(8,128)(2,1)S(1)} %collective-permute-done.18.refs_0_, bf16[32,6144]{1,0:T(8,128)(2,1)S(1)} %collective-permute-done.19.refs_1_, bf16[32,6144]{1,0:T(8,128)(2,1)S(1)} %collective-permute-done.20.refs_2_, ...), custom_call_target="tpu_custom_call" | custom-call | flops 2415919104 | bytes 12582912 | tf_op jit(solution)/shard_map/pallas_call | solution.py:133
  154.9 7.3 %collective-permute-done.21 = bf16[512,384]{1,0:T(8,128)(2,1)} collective-permute-done((bf16[512,384]{1,0:T(8,128)(2,1)}, bf16[512,384]{1,0:T(8,128)(2,1)}, u32[]{:S(2)}, u32[]{:S(2)}) %collective-permute-start.21) | collective-permute-done | bytes 393248 | tf_op jit(solution)/shard_map/ppermute | solution.py:36
  162.2 2.9 %collective-permute-done.24 = bf16[512,384]{1,0:T(8,128)(2,1)S(1)} collective-permute-done((bf16[512,384]{1,0:T(8,128)(2,1)}, bf16[512,384]{1,0:T(8,128)(2,1)S(1)}, u32[]{:S(2)}, u32[]{:S(2)}) %collective-permute-start.24) | collective-permute-done | bytes 393248 | tf_op jit(solution)/shard_map/ppermute | solution.py:40
  168.2 3.8 %fusion.14 = f32[768,384]{1,0:T(8,128)S(1)} fusion(bf16[2048,768]{1,0:T(8,128)(2,1)} %all-gather.3.cloned.1.call-done, bf16[2048,384]{1,0:T(8,128)(2,1)S(1)} %bitcast.77), kind=kOutput, calls=%fused_computation.47 | convolution fusion | flops 1207959552 | bytes 5898240 | tf_op jit(solution)/shard_map/dot_general | solution.py:100
  176.0 10.4 %collective-permute-done.27 = bf16[512,384]{1,0:T(8,128)(2,1)} collective-permute-done((bf16[512,384]{1,0:T(8,128)(2,1)}, bf16[512,384]{1,0:T(8,128)(2,1)}, u32[]{:S(2)}, u32[]{:S(2)}) %collective-permute-start.27) | collective-permute-done | bytes 393248 | tf_op jit(solution)/shard_map/ppermute | solution.py:40
  186.4 1.4 pad_maximum_fusion.1
  187.9 3.7 %fusion.15 = f32[768,384]{1,0:T(8,128)S(1)} fusion(bf16[2048,768]{1,0:T(8,128)(2,1)} %all-gather.5.cloned.1.call-done, bf16[2048,384]{1,0:T(8,128)(2,1)S(1)} %bitcast.78), kind=kOutput, calls=%fused_computation.48 | convolution fusion | flops 1207959552 | bytes 5898240 | tf_op jit(solution)/shard_map/dot_general | solution.py:100
  192.4 1.6 collective-permute-done.29
  (99 shorter events, 27.3 us)
Async XLA Ops:
  7.2 161.0 %all-gather.3.cloned.1.call-start = ((), (), s32[]{:S(2)}) async-start(), calls=%async_computation.1 | async-start | bytes 3932160 | tf_op jit(solution)/shard_map/all_gather | solution.py:96
  8.9 8.4 %collective-permute-start = (bf16[2,128,384]{2,1,0:T(8,128)(2,1)S(1)}, bf16[2,128,384]{2,1,0:T(8,128)(2,1)S(1)}, u32[]{:S(2)}, u32[]{:S(2)}) collective-permute-start(bf16[2,128,384]{2,1,0:T(8,128)(2,1)S(1)} %get-tuple-element.114), channel_id=1, source_target_pairs={{0,1},{1,0},{2,3},{3,2},{4,5},{5,4},{6,7},{7,6},{8,9},{9,8},{10,11... | collective-permute-start | bytes 589832 | tf_op jit(solution)/shard_map/ppermute | solution.py:32
  17.2 3.5 %collective-permute-start.1 = (bf16[128,6144]{1,0:T(8,128)(2,1)S(1)}, bf16[128,6144]{1,0:T(8,128)(2,1)S(1)}, u32[]{:S(2)}, u32[]{:S(2)}) collective-permute-start(bf16[128,6144]{1,0:T(8,128)(2,1)S(1)} %get-tuple-element.52), channel_id=1, source_target_pairs={{0,1},{1,0},{2,3},{3,2},{4,5},{5,4},{6,7},{7,6},{8,9},{9,8},{10,11... | collective-permute-start | bytes 4718600 | tf_op jit(solution)/shard_map/ppermute | solution.py:32
  17.4 10.7 %collective-permute-start.7 = (bf16[2,128,768]{2,1,0:T(8,128)(2,1)S(1)}, bf16[2,128,768]{2,1,0:T(8,128)(2,1)S(1)}, u32[]{:S(2)}, u32[]{:S(2)}) collective-permute-start(bf16[2,128,768]{2,1,0:T(8,128)(2,1)S(1)} %get-tuple-element.111), channel_id=1, source_target_pairs={{0,64},{16,80},{32,96},{48,112},{64,0},{80,16},{96,32},{112,48},{1... | collective-permute-start | bytes 1179656 | tf_op jit(solution)/shard_map/ppermute | solution.py:167
  21.2 20.3 %collective-permute-start.2 = (bf16[32,6144]{1,0:T(8,128)(2,1)S(1)}, bf16[32,6144]{1,0:T(8,128)(2,1)S(1)}, u32[]{:S(2)}, u32[]{:S(2)}) collective-permute-start(bf16[32,6144]{1,0:T(8,128)(2,1)S(1)} %get-tuple-element.104), channel_id=1, source_target_pairs={{0,2},{1,3},{2,4},{3,5},{4,6},{5,7},{6,0},{7,1},{8,10},{9,11},{10,... | collective-permute-start | bytes 1179656 | tf_op jit(solution)/shard_map/ppermute | solution.py:40
  21.3 20.2 %collective-permute-start.3 = (bf16[32,6144]{1,0:T(8,128)(2,1)S(1)}, bf16[32,6144]{1,0:T(8,128)(2,1)S(1)}, u32[]{:S(2)}, u32[]{:S(2)}) collective-permute-start(bf16[32,6144]{1,0:T(8,128)(2,1)S(1)} %get-tuple-element.106), channel_id=1, source_target_pairs={{0,4},{1,5},{2,6},{3,7},{4,0},{5,1},{6,2},{7,3},{8,12},{9,13},{10,... | collective-permute-start | bytes 1179656 | tf_op jit(solution)/shard_map/ppermute | solution.py:40
  23.2 18.6 %collective-permute-start.4 = (bf16[32,6144]{1,0:T(8,128)(2,1)S(1)}, bf16[32,6144]{1,0:T(8,128)(2,1)S(1)}, u32[]{:S(2)}, u32[]{:S(2)}) collective-permute-start(bf16[32,6144]{1,0:T(8,128)(2,1)S(1)} %get-tuple-element.105), channel_id=1, source_target_pairs={{0,6},{1,7},{2,0},{3,1},{4,2},{5,3},{6,4},{7,5},{8,14},{9,15},{10,... | collective-permute-start | bytes 1179656 | tf_op jit(solution)/shard_map/ppermute | solution.py:40
  27.0 15.0 %collective-permute-start.5 = (bf16[128,6144]{1,0:T(8,128)(2,1)S(1)}, bf16[128,6144]{1,0:T(8,128)(2,1)S(1)}, u32[]{:S(2)}, u32[]{:S(2)}) collective-permute-start(bf16[128,6144]{1,0:T(8,128)(2,1)S(1)} %get-tuple-element.56), channel_id=1, source_target_pairs={{0,1},{1,0},{2,3},{3,2},{4,5},{5,4},{6,7},{7,6},{8,9},{9,8},{10,11... | collective-permute-start | bytes 4718600 | tf_op jit(solution)/shard_map/ppermute | solution.py:32
  28.9 23.1 %collective-permute-start.8 = (bf16[2,128,768]{2,1,0:T(8,128)(2,1)S(1)}, bf16[2,128,768]{2,1,0:T(8,128)(2,1)S(1)}, u32[]{:S(2)}, u32[]{:S(2)}) collective-permute-start(bf16[2,128,768]{2,1,0:T(8,128)(2,1)S(1)} %get-tuple-element.110), channel_id=1, source_target_pairs={{0,128},{16,144},{32,160},{48,176},{64,192},{80,208},{96,224},{112... | collective-permute-start | bytes 1179656 | tf_op jit(solution)/shard_map/ppermute | solution.py:91
  42.5 11.0 %collective-permute-start.10 = (bf16[32,6144]{1,0:T(8,128)(2,1)S(1)}, bf16[32,6144]{1,0:T(8,128)(2,1)S(1)}, u32[]{:S(2)}, u32[]{:S(2)}) collective-permute-start(bf16[32,6144]{1,0:T(8,128)(2,1)S(1)} %get-tuple-element.101), channel_id=1, source_target_pairs={{0,4},{1,5},{2,6},{3,7},{4,0},{5,1},{6,2},{7,3},{8,12},{9,13},{10,... | collective-permute-start | bytes 1179656 | tf_op jit(solution)/shard_map/ppermute | solution.py:40
  43.6 19.9 %collective-permute-start.11 = (bf16[32,6144]{1,0:T(8,128)(2,1)S(1)}, bf16[32,6144]{1,0:T(8,128)(2,1)S(1)}, u32[]{:S(2)}, u32[]{:S(2)}) collective-permute-start(bf16[32,6144]{1,0:T(8,128)(2,1)S(1)} %get-tuple-element.100), channel_id=1, source_target_pairs={{0,6},{1,7},{2,0},{3,1},{4,2},{5,3},{6,4},{7,5},{8,14},{9,15},{10,... | collective-permute-start | bytes 1179656 | tf_op jit(solution)/shard_map/ppermute | solution.py:40
  46.1 17.4 %collective-permute-start.9 = (bf16[32,6144]{1,0:T(8,128)(2,1)S(1)}, bf16[32,6144]{1,0:T(8,128)(2,1)S(1)}, u32[]{:S(2)}, u32[]{:S(2)}) collective-permute-start(bf16[32,6144]{1,0:T(8,128)(2,1)S(1)} %get-tuple-element.102), channel_id=1, source_target_pairs={{0,2},{1,3},{2,4},{3,5},{4,6},{5,7},{6,0},{7,1},{8,10},{9,11},{10,... | collective-permute-start | bytes 1179656 | tf_op jit(solution)/shard_map/ppermute | solution.py:40
  46.3 17.3 %collective-permute-start.6 = (bf16[32,6144]{1,0:T(8,128)(2,1)S(1)}, bf16[32,6144]{1,0:T(8,128)(2,1)S(1)}, u32[]{:S(2)}, u32[]{:S(2)}) collective-permute-start(bf16[32,6144]{1,0:T(8,128)(2,1)S(1)} %add_convert_fusion.2), channel_id=1, source_target_pairs={{0,8},{1,9},{2,10},{3,11},{4,12},{5,13},{6,14},{7,15},{8,0},{9,1},... | collective-permute-start | bytes 1179656 | tf_op jit(solution)/shard_map/ppermute | solution.py:36
  66.0 34.6 %collective-permute-start.13 = (bf16[384,6144]{1,0:T(8,128)(2,1)}, bf16[384,6144]{1,0:T(8,128)(2,1)}, u32[]{:S(2)}, u32[]{:S(2)}) collective-permute-start(bf16[384,6144]{1,0:T(8,128)(2,1)} %refs_8_.1), channel_id=1, source_target_pairs={{0,1},{1,0},{2,3},{3,2},{4,5},{5,4},{6,7},{7,6},{8,9},{9,8},{10,11... | collective-permute-start | bytes 14155784 | tf_op jit(solution)/shard_map/ppermute | solution.py:32
  67.3 15.3 %collective-permute-start.12 = (bf16[32,6144]{1,0:T(8,128)(2,1)S(1)}, bf16[32,6144]{1,0:T(8,128)(2,1)S(1)}, u32[]{:S(2)}, u32[]{:S(2)}) collective-permute-start(bf16[32,6144]{1,0:T(8,128)(2,1)S(1)} %get-tuple-element.67.refs_7_), channel_id=1, source_target_pairs={{0,8},{1,9},{2,10},{3,11},{4,12},{5,13},{6,14},{7,15},{8,0},{9,1},... | collective-permute-start | bytes 1179656 | tf_op jit(solution)/shard_map/ppermute | solution.py:36
  72.6 24.2 %collective-permute-start.14 = (bf16[32,6144]{1,0:T(8,128)(2,1)S(1)}, bf16[32,6144]{1,0:T(8,128)(2,1)S(1)}, u32[]{:S(2)}, u32[]{:S(2)}) collective-permute-start(bf16[32,6144]{1,0:T(8,128)(2,1)S(1)} %get-tuple-element.67.refs_7_), channel_id=1, source_target_pairs={{0,6},{1,7},{2,0},{3,1},{4,2},{5,3},{6,4},{7,5},{8,14},{9,15},{10,... | collective-permute-start | bytes 1179656 | tf_op jit(solution)/shard_map/ppermute | solution.py:40
  80.1 16.7 %collective-permute-start.15 = (bf16[32,6144]{1,0:T(8,128)(2,1)S(1)}, bf16[32,6144]{1,0:T(8,128)(2,1)S(1)}, u32[]{:S(2)}, u32[]{:S(2)}) collective-permute-start(bf16[32,6144]{1,0:T(8,128)(2,1)S(1)} %get-tuple-element.67.refs_7_), channel_id=1, source_target_pairs={{0,4},{1,5},{2,6},{3,7},{4,0},{5,1},{6,2},{7,3},{8,12},{9,13},{10,... | collective-permute-start | bytes 1179656 | tf_op jit(solution)/shard_map/ppermute | solution.py:40
  80.1 20.5 %collective-permute-start.16 = (bf16[32,6144]{1,0:T(8,128)(2,1)S(1)}, bf16[32,6144]{1,0:T(8,128)(2,1)S(1)}, u32[]{:S(2)}, u32[]{:S(2)}) collective-permute-start(bf16[32,6144]{1,0:T(8,128)(2,1)S(1)} %get-tuple-element.67.refs_7_), channel_id=1, source_target_pairs={{0,2},{1,3},{2,4},{3,5},{4,6},{5,7},{6,0},{7,1},{8,10},{9,11},{10,... | collective-permute-start | bytes 1179656 | tf_op jit(solution)/shard_map/ppermute | solution.py:40
  101.7 36.4 %all-to-all-start = ((bf16[16,32,384]{2,1,0:T(8,128)(2,1)}), bf16[16,32,384]{2,1,0:T(8,128)(2,1)}, u32[]{:S(2)}, u32[]{:S(2)}) async-start(bf16[16,32,384]{2,1,0:T(8,128)(2,1)} %bitcast.28), calls=%async_computation | async-start | bytes 786432 | tf_op jit(solution)/shard_map/all_to_all | solution.py:200
  108.0 79.9 %all-gather.5.cloned.1.call-start = ((), (), s32[]{:S(2)}) async-start(), calls=%async_computation.2 | async-start | bytes 3932160 | tf_op jit(solution)/shard_map/all_gather | solution.py:96
  108.0 28.0 %collective-permute-start.17 = (bf16[2,128,768]{2,1,0:T(8,128)(2,1)}, bf16[2,128,768]{2,1,0:T(8,128)(2,1)}, u32[]{:S(2)}, u32[]{:S(2)}) collective-permute-start(bf16[2,128,768]{2,1,0:T(8,128)(2,1)} %get-tuple-element.68), channel_id=1, source_target_pairs={{0,128},{16,144},{32,160},{48,176},{64,192},{80,208},{96,224},{112... | collective-permute-start | bytes 1179656 | tf_op jit(solution)/shard_map/ppermute | solution.py:91
  110.3 31.9 %collective-permute-start.18 = (bf16[32,6144]{1,0:T(8,128)(2,1)S(1)}, bf16[32,6144]{1,0:T(8,128)(2,1)S(1)}, u32[]{:S(2)}, u32[]{:S(2)}) collective-permute-start(bf16[32,6144]{1,0:T(8,128)(2,1)S(1)} %collective-permute-done.12.refs_3_), channel_id=1, source_target_pairs={{0,6},{1,7},{2,0},{3,1},{4,2},{5,3},{6,4},{7,5},{8,14},{9,15},{10,... | collective-permute-start | bytes 1179656 | tf_op jit(solution)/shard_map/ppermute | solution.py:40
  110.3 31.9 %collective-permute-start.19 = (bf16[32,6144]{1,0:T(8,128)(2,1)S(1)}, bf16[32,6144]{1,0:T(8,128)(2,1)S(1)}, u32[]{:S(2)}, u32[]{:S(2)}) collective-permute-start(bf16[32,6144]{1,0:T(8,128)(2,1)S(1)} %collective-permute-done.12.refs_3_), channel_id=1, source_target_pairs={{0,4},{1,5},{2,6},{3,7},{4,0},{5,1},{6,2},{7,3},{8,12},{9,13},{10,... | collective-permute-start | bytes 1179656 | tf_op jit(solution)/shard_map/ppermute | solution.py:40
  111.0 31.2 %collective-permute-start.20 = (bf16[32,6144]{1,0:T(8,128)(2,1)S(1)}, bf16[32,6144]{1,0:T(8,128)(2,1)S(1)}, u32[]{:S(2)}, u32[]{:S(2)}) collective-permute-start(bf16[32,6144]{1,0:T(8,128)(2,1)S(1)} %collective-permute-done.12.refs_3_), channel_id=1, source_target_pairs={{0,2},{1,3},{2,4},{3,5},{4,6},{5,7},{6,0},{7,1},{8,10},{9,11},{10,... | collective-permute-start | bytes 1179656 | tf_op jit(solution)/shard_map/ppermute | solution.py:40
  142.4 19.8 %collective-permute-start.21 = (bf16[512,384]{1,0:T(8,128)(2,1)}, bf16[512,384]{1,0:T(8,128)(2,1)}, u32[]{:S(2)}, u32[]{:S(2)}) collective-permute-start(bf16[512,384]{1,0:T(8,128)(2,1)} %bitcast.82), channel_id=1, source_target_pairs={{0,8},{1,9},{2,10},{3,11},{4,12},{5,13},{6,14},{7,15},{8,0},{9,1},... | collective-permute-start | bytes 1179656 | tf_op jit(solution)/shard_map/ppermute | solution.py:36
  143.1 19.1 %collective-permute-start.22 = (bf16[512,384]{1,0:T(8,128)(2,1)}, bf16[512,384]{1,0:T(8,128)(2,1)S(1)}, u32[]{:S(2)}, u32[]{:S(2)}) collective-permute-start(bf16[512,384]{1,0:T(8,128)(2,1)} %bitcast.83), channel_id=1, source_target_pairs={{0,6},{1,7},{2,0},{3,1},{4,2},{5,3},{6,4},{7,5},{8,14},{9,15},{10,... | collective-permute-start | bytes 1179656 | tf_op jit(solution)/shard_map/ppermute | solution.py:40
  144.5 17.7 %collective-permute-start.23 = (bf16[512,384]{1,0:T(8,128)(2,1)}, bf16[512,384]{1,0:T(8,128)(2,1)S(1)}, u32[]{:S(2)}, u32[]{:S(2)}) collective-permute-start(bf16[512,384]{1,0:T(8,128)(2,1)} %bitcast.84), channel_id=1, source_target_pairs={{0,4},{1,5},{2,6},{3,7},{4,0},{5,1},{6,2},{7,3},{8,12},{9,13},{10,... | collective-permute-start | bytes 1179656 | tf_op jit(solution)/shard_map/ppermute | solution.py:40
  144.5 20.6 %collective-permute-start.24 = (bf16[512,384]{1,0:T(8,128)(2,1)}, bf16[512,384]{1,0:T(8,128)(2,1)S(1)}, u32[]{:S(2)}, u32[]{:S(2)}) collective-permute-start(bf16[512,384]{1,0:T(8,128)(2,1)} %bitcast.85), channel_id=1, source_target_pairs={{0,2},{1,3},{2,4},{3,5},{4,6},{5,7},{6,0},{7,1},{8,10},{9,11},{10,... | collective-permute-start | bytes 1179656 | tf_op jit(solution)/shard_map/ppermute | solution.py:40
  165.1 10.2 %collective-permute-start.25 = (bf16[512,384]{1,0:T(8,128)(2,1)}, bf16[512,384]{1,0:T(8,128)(2,1)S(1)}, u32[]{:S(2)}, u32[]{:S(2)}) collective-permute-start(bf16[512,384]{1,0:T(8,128)(2,1)} %collective-permute-done.21), channel_id=1, source_target_pairs={{0,6},{1,7},{2,0},{3,1},{4,2},{5,3},{6,4},{7,5},{8,14},{9,15},{10,... | collective-permute-start | bytes 1179656 | tf_op jit(solution)/shard_map/ppermute | solution.py:40
  165.1 10.9 %collective-permute-start.26 = (bf16[512,384]{1,0:T(8,128)(2,1)}, bf16[512,384]{1,0:T(8,128)(2,1)}, u32[]{:S(2)}, u32[]{:S(2)}) collective-permute-start(bf16[512,384]{1,0:T(8,128)(2,1)} %collective-permute-done.21), channel_id=1, source_target_pairs={{0,4},{1,5},{2,6},{3,7},{4,0},{5,1},{6,2},{7,3},{8,12},{9,13},{10,... | collective-permute-start | bytes 1179656 | tf_op jit(solution)/shard_map/ppermute | solution.py:40
  165.8 20.6 %collective-permute-start.27 = (bf16[512,384]{1,0:T(8,128)(2,1)}, bf16[512,384]{1,0:T(8,128)(2,1)}, u32[]{:S(2)}, u32[]{:S(2)}) collective-permute-start(bf16[512,384]{1,0:T(8,128)(2,1)} %collective-permute-done.21), channel_id=1, source_target_pairs={{0,2},{1,3},{2,4},{3,5},{4,6},{5,7},{6,0},{7,1},{8,10},{9,11},{10,... | collective-permute-start | bytes 1179656 | tf_op jit(solution)/shard_map/ppermute | solution.py:40
  166.7 5.3 %collective-permute-start.28 = (bf16[256,384]{1,0:T(8,128)(2,1)}, bf16[256,384]{1,0:T(8,128)(2,1)}, u32[]{:S(2)}, u32[]{:S(2)}) collective-permute-start(bf16[256,384]{1,0:T(8,128)(2,1)} %get-tuple-element.87), channel_id=1, source_target_pairs={{0,1},{1,0},{2,3},{3,2},{4,5},{5,4},{6,7},{7,6},{8,9},{9,8},{10,11... | collective-permute-start | bytes 589832 | tf_op jit(solution)/shard_map/ppermute | solution.py:32
  (11 other events, 135.0 us)
Sparse Core Ops, SparseCore 0:
  67.4 51.2 all-gather.2
  142.4 37.9 all-gather.4
